TPU v7x, 32 devices: a whole 2x2x4 slice. The times are simulated.
32 devices in a mesh: yz: 8 (over y, x, core), gx: 4 (over z).
Axes of the slice: x: 2, y: 2, z: 4, core: 2. Of those that a mesh axis runs over, the one named last changes fastest.
Arguments:
- state: float32 [7, 64, 64, 128], P(None, 'gx', 'yz'), may hold values from -2.5 to 2.5
- register: float32 [7, 64, 64, 128], P(None, 'gx', 'yz'), may hold values from -3 to 3
- forcing: float32 [3, 64, 64, 128], P(None, 'gx', 'yz'), may hold values from -3 to 3
- y_shift: int32 [1], replicated, may hold values from 0 to 63
Outputs:
- new_state: float32 [7, 64, 64, 128], P(None, 'gx', 'yz')
- new_register: float32 [7, 64, 64, 128], P(None, 'gx', 'yz')
All inputs are finite; a program needn't handle non-finite values.
Results may differ from a plain program's by a relative error of at most 0.000092.
Values sent between devices are 32-bit elements; how exact they have to be, the bound alone decides.
No kernel may reach another device: no remote copies, remote signals or barrier semaphores. Data moves between devices by JAX's collectives and lax.ppermute only.
A program may use at most 64 MiB of HBM per device.

v0:
```python
import jax
import jax.numpy as jnp
from jax import lax
from jax.sharding import PartitionSpec as P


def padded_2(block, sides, width):
    for axis, dim in sides:
        count = lax.axis_size(axis)
        forward = [(i, i + 1) for i in range(count - 1)]
        forward.append((count - 1, 0))
        backward = [(target, source) for source, target in forward]
        low = lax.ppermute(
            lax.slice_in_dim(block, block.shape[dim] - width, None, axis=dim), axis, forward
        )
        high = lax.ppermute(lax.slice_in_dim(block, 0, width, axis=dim), axis, backward)
        block = jnp.concatenate([low, block, high], axis=dim)
    return block


def passed_along(value, axis, by):
    peers = lax.axis_size(axis)
    return lax.ppermute(value, axis, [(i, (i + by) % peers) for i in range(peers)])


def first_diff(field, axis):
    count = field.shape[axis] - 6

    def part(offset):
        return lax.slice_in_dim(field, 3 + offset, 3 + offset + count, axis=axis)

    return (45.0 * (part(1) - part(-1)) - 9.0 * (part(2) - part(-2)) + (part(3) - part(-3))) / 60.0


def second_diff(field, axis):
    count = field.shape[axis] - 6

    def part(offset):
        return lax.slice_in_dim(field, 3 + offset, 3 + offset + count, axis=axis)

    return (
        -490.0 * part(0)
        + 270.0 * (part(1) + part(-1))
        - 27.0 * (part(2) + part(-2))
        + 2.0 * (part(3) + part(-3))
    ) / 180.0


def inner(field, axes):
    for axis in axes:
        field = lax.slice_in_dim(field, 3, field.shape[axis] - 3, axis=axis)
    return field


def tendency(padded, forcing, xfrac, inv_width):
    grads = [
        inner(first_diff(padded, 1), (2, 3)),
        inner(first_diff(padded, 2), (1, 3)),
        inner(first_diff(padded, 3), (1, 2)),
    ]
    vectors = padded[:6]
    curv = [
        inner(second_diff(vectors, 1), (2, 3)),
        inner(second_diff(vectors, 2), (1, 3)),
        inner(second_diff(vectors, 3), (1, 2)),
    ]
    cross_xy = inner(first_diff(first_diff(vectors, 2), 1), (3,))
    cross_xz = inner(first_diff(first_diff(vectors, 3), 1), (2,))
    cross_yz = inner(first_diff(first_diff(vectors, 3), 2), (1,))
    center = inner(padded, (1, 2, 3))
    velx, vely, velz = (center[0], center[1], center[2])
    potx, poty = (center[3], center[4])

    def grad(axis, comp):
        return grads[axis][comp]

    def lapl(comp):
        return curv[0][comp] + curv[1][comp] + curv[2][comp]

    def grad_div(first):
        return (
            curv[0][first] + cross_xy[first + 1] + cross_xz[first + 2],
            cross_xy[first] + curv[1][first + 1] + cross_yz[first + 2],
            cross_xz[first] + cross_yz[first + 1] + curv[2][first + 2],
        )

    fieldx = grad(1, 5) - grad(2, 4)
    fieldy = grad(2, 3) - grad(0, 5)
    fieldz = grad(0, 4) - grad(1, 3) + 0.5
    potdiv = grad_div(3)
    currx = potdiv[0] - lapl(3)
    curry = potdiv[1] - lapl(4)
    currz = potdiv[2] - lapl(5)
    veldiv = grad_div(0)
    inv_rho = jnp.exp(-center[6])
    flow = -1.5 * xfrac
    shear_rate = -1.5 * inv_width

    def advect(comp):
        return velx * grad(0, comp) + (vely + flow) * grad(1, comp) + velz * grad(2, comp)

    divu = grad(0, 0) + grad(1, 1) + grad(2, 2)
    lorentz = (
        curry * fieldz - currz * fieldy,
        currz * fieldx - currx * fieldz,
        currx * fieldy - curry * fieldx,
    )
    emf = (
        vely * fieldz - velz * fieldy,
        velz * fieldx - velx * fieldz,
        velx * fieldy - vely * fieldx,
    )
    curr = (currx, curry, currz)
    rates = []
    for comp in range(3):
        rate = -advect(comp) - grad(comp, 6) + lorentz[comp] * inv_rho
        total = jnp.zeros_like(velx)
        for col in range(3):
            strain = 0.5 * (grad(col, comp) + grad(comp, col))
            if col == comp:
                strain = strain - divu / 3.0
            total = total + 2.0 * strain * grad(col, 6)
        rate = rate + 0.05 * (lapl(comp) + veldiv[comp] / 3.0 + total) + forcing[comp]
        if comp == 0:
            rate = rate + 2.0 * 0.5 * vely
        if comp == 1:
            rate = rate - 2.0 * 0.5 * velx - shear_rate * velx
        rates.append(rate)
    for comp in range(3):
        rate = emf[comp] - flow * grad(1, 3 + comp) - 0.05 * curr[comp]
        if comp == 0:
            rate = rate - shear_rate * poty
        rates.append(rate)
    rates.append(-advect(6) - divu)
    return jnp.stack(rates)


def per_device(state, register, forcing, y_shift):
    cells_x = state.shape[1]
    cells_y = state.shape[2]
    slabs_x = lax.axis_size("gx")
    slabs_y = lax.axis_size("yz")
    total_x = cells_x * slabs_x
    total_y = cells_y * slabs_y
    where_x = lax.axis_index("gx")
    extended = padded_2(state, (("gx", 1),), 3)
    lower = extended[:, :3]
    upper = extended[:, cells_x + 3 :]
    at_low = where_x == 0
    at_high = where_x == slabs_x - 1
    boundary = jnp.where(at_high, upper, lower)
    offset = y_shift[0]
    amount = jnp.where(at_high, total_y - offset, offset) % total_y
    whole_steps = amount // cells_y
    remainder = amount % cells_y
    levels = slabs_y.bit_length() - 1
    bit_list = list(range(levels))
    current = boundary
    for bit in bit_list:
        moved = passed_along(current, "yz", slabs_y - (1 << bit))
        current = jnp.where(whole_steps >> bit & 1 == 1, moved, current)
    following = passed_along(current, "yz", slabs_y - 1)
    joined = jnp.concatenate([current, following], axis=2)
    sheared = lax.dynamic_slice_in_dim(joined, remainder, cells_y, 2)
    lower = jnp.where(at_low, sheared, lower)
    upper = jnp.where(at_high, sheared, upper)
    extended = jnp.concatenate([lower, extended[:, 3 : cells_x + 3], upper], axis=1)
    padded = padded_2(extended, (("yz", 2),), 3)
    padded = jnp.concatenate([padded[:, :, :, -3:], padded, padded[:, :, :, :3]], axis=3)
    inv_width = 1.0 / total_x
    index = (where_x * cells_x + jnp.arange(cells_x)).astype(jnp.float32)
    xfrac = ((index + 0.5) * inv_width - 0.5).reshape(cells_x, 1, 1)
    rate = tendency(padded, forcing, xfrac, inv_width)
    new_register = -5.0 / 9.0 * register + 0.15 * rate
    new_state = state + 15.0 / 16.0 * new_register
    return (new_state, new_register)


def solution(mesh):
    return jax.shard_map(
        per_device,
        mesh=mesh,
        in_specs=(
            P(None, "gx", "yz", None),
            P(None, "gx", "yz", None),
            P(None, "gx", "yz", None),
            P(),
        ),
        out_specs=(P(None, "gx", "yz", None), P(None, "gx", "yz", None)),
        check_vma=False,
    )
```

profile of v0, /device:TPU:0, one launch (start us, length us, event | category | flops | bytes accessed | tf_op | source)
XLA Modules:
  0.0 56.8 jit_solution(6710785325214899462)
XLA Ops:
  0.6 1.1 %copy.51 = f32[7,16,8,128]{3,1,2,0:T(8,128)S(1)} copy(f32[7,16,8,128]{3,2,1,0:T(8,128)} %param.4) | data formatting | bytes 917504 | tf_op args[0]
  1.8 3.1 %collective-permute-start.1 = (f32[7,3,8,128]{3,1,2,0:T(4,128)S(1)}, f32[7,3,8,128]{3,1,2,0:T(4,128)S(1)}, u32[]{:S(2)}, u32[]{:S(2)}) collective-permute-start(f32[7,3,8,128]{3,1,2,0:T(4,128)S(1)} %get-tuple-element.29), channel_id=1, source_target_pairs={{0,1},{1,2},{2,3},{3,0},{4,5},{5,6},{6,7},{7,4},{8,9},{9,10},{10,1... | collective-permute-start | bytes 258056 | tf_op jit(solution)/shard_map/ppermute | solution.py:13
  4.9 2.1 %collective-permute-start = (f32[7,3,8,128]{3,1,2,0:T(4,128)S(1)}, f32[7,3,8,128]{3,1,2,0:T(4,128)S(1)}, u32[]{:S(2)}, u32[]{:S(2)}) collective-permute-start(f32[7,3,8,128]{3,1,2,0:T(4,128)S(1)} %get-tuple-element.30), channel_id=1, source_target_pairs={{1,0},{2,1},{3,2},{0,3},{5,4},{6,5},{7,6},{4,7},{9,8},{10,9},{11,1... | collective-permute-start | bytes 258056 | tf_op jit(solution)/shard_map/ppermute | solution.py:16
  7.0 3.9 %collective-permute-done.1 = f32[7,3,8,128]{3,1,2,0:T(4,128)S(1)} collective-permute-done((f32[7,3,8,128]{3,1,2,0:T(4,128)S(1)}, f32[7,3,8,128]{3,1,2,0:T(4,128)S(1)}, u32[]{:S(2)}, u32[]{:S(2)}) %collective-permute-start.1) | collective-permute-done | bytes 86048 | tf_op jit(solution)/shard_map/ppermute | solution.py:13
  10.9 1.1 %collective-permute-done = f32[7,3,8,128]{3,1,2,0:T(4,128)S(1)} collective-permute-done((f32[7,3,8,128]{3,1,2,0:T(4,128)S(1)}, f32[7,3,8,128]{3,1,2,0:T(4,128)S(1)}, u32[]{:S(2)}, u32[]{:S(2)}) %collective-permute-start) | collective-permute-done | bytes 86048 | tf_op jit(solution)/shard_map/ppermute | solution.py:16
  12.0 1.5 %collective-permute-start.2 = (f32[7,3,8,128]{3,1,2,0:T(4,128)S(1)}, f32[7,3,8,128]{3,1,2,0:T(4,128)S(1)}, u32[]{:S(2)}, u32[]{:S(2)}) collective-permute-start(f32[7,3,8,128]{3,1,2,0:T(4,128)S(1)} %broadcast_select_fusion.1), channel_id=1, source_target_pairs={{0,28},{4,0},{8,4},{12,8},{16,12},{20,16},{24,20},{28,24},{1,29},{... | collective-permute-start | bytes 258056 | tf_op jit(solution)/shard_map/ppermute | solution.py:23
  14.2 1.7 %collective-permute-done.2 = f32[7,3,8,128]{3,1,2,0:T(4,128)S(1)} collective-permute-done((f32[7,3,8,128]{3,1,2,0:T(4,128)S(1)}, f32[7,3,8,128]{3,1,2,0:T(4,128)S(1)}, u32[]{:S(2)}, u32[]{:S(2)}) %collective-permute-start.2) | collective-permute-done | bytes 86048 | tf_op jit(solution)/shard_map/ppermute | solution.py:23
  15.9 0.0 copy-start.2
  15.9 1.1 %collective-permute-start.3 = (f32[7,3,8,128]{3,1,2,0:T(4,128)S(1)}, f32[7,3,8,128]{3,1,2,0:T(4,128)S(1)}, u32[]{:S(2)}, u32[]{:S(2)}) collective-permute-start(f32[7,3,8,128]{3,1,2,0:T(4,128)S(1)} %broadcast_select_fusion.2), channel_id=1, source_target_pairs={{0,24},{4,28},{8,0},{12,4},{16,8},{20,12},{24,16},{28,20},{1,25},{... | collective-permute-start | bytes 258056 | tf_op jit(solution)/shard_map/ppermute | solution.py:23
  16.9 4.5 %collective-permute-done.3 = f32[7,3,8,128]{3,1,2,0:T(4,128)S(1)} collective-permute-done((f32[7,3,8,128]{3,1,2,0:T(4,128)S(1)}, f32[7,3,8,128]{3,1,2,0:T(4,128)S(1)}, u32[]{:S(2)}, u32[]{:S(2)}) %collective-permute-start.3) | collective-permute-done | bytes 86048 | tf_op jit(solution)/shard_map/ppermute | solution.py:23
  21.5 0.7 %collective-permute-start.4 = (f32[7,3,8,128]{3,1,2,0:T(4,128)S(1)}, f32[7,3,8,128]{3,1,2,0:T(4,128)S(1)}, u32[]{:S(2)}, u32[]{:S(2)}) collective-permute-start(f32[7,3,8,128]{3,1,2,0:T(4,128)S(1)} %broadcast_select_fusion.3), channel_id=1, source_target_pairs={{0,16},{4,20},{8,24},{12,28},{16,0},{20,4},{24,8},{28,12},{1,17},{... | collective-permute-start | bytes 258056 | tf_op jit(solution)/shard_map/ppermute | solution.py:23
  22.1 4.2 %collective-permute-done.4 = f32[7,3,8,128]{3,1,2,0:T(4,128)S(1)} collective-permute-done((f32[7,3,8,128]{3,1,2,0:T(4,128)S(1)}, f32[7,3,8,128]{3,1,2,0:T(4,128)S(1)}, u32[]{:S(2)}, u32[]{:S(2)}) %collective-permute-start.4) | collective-permute-done | bytes 86048 | tf_op jit(solution)/shard_map/ppermute | solution.py:23
  26.4 2.2 %collective-permute-start.5 = (f32[7,3,8,128]{3,1,2,0:T(4,128)S(1)}, f32[7,3,8,128]{3,1,2,0:T(4,128)S(1)}, u32[]{:S(2)}, u32[]{:S(2)}) collective-permute-start(f32[7,3,8,128]{3,1,2,0:T(4,128)S(1)} %broadcast_select_fusion.4), channel_id=1, source_target_pairs={{0,28},{4,0},{8,4},{12,8},{16,12},{20,16},{24,20},{28,24},{1,29},{... | collective-permute-start | bytes 258056 | tf_op jit(solution)/shard_map/ppermute | solution.py:23
  28.5 2.4 %collective-permute-done.5 = f32[7,3,8,128]{3,1,2,0:T(4,128)S(1)} collective-permute-done((f32[7,3,8,128]{3,1,2,0:T(4,128)S(1)}, f32[7,3,8,128]{3,1,2,0:T(4,128)S(1)}, u32[]{:S(2)}, u32[]{:S(2)}) %collective-permute-start.5) | collective-permute-done | bytes 86048 | tf_op jit(solution)/shard_map/ppermute | solution.py:23
  30.9 0.1 broadcast_select_fusion.5
  31.0 0.1 pad_maximum_fusion.5
  31.1 2.8 %collective-permute-start.7 = (f32[7,22,3,128]{3,1,2,0:T(8,128)S(1)}, f32[7,22,3,128]{3,1,2,0:T(8,128)S(1)}, u32[]{:S(2)}, u32[]{:S(2)}) collective-permute-start(f32[7,22,3,128]{3,1,2,0:T(8,128)S(1)} %get-tuple-element.28), channel_id=1, source_target_pairs={{4,0},{8,4},{12,8},{16,12},{20,16},{24,20},{28,24},{0,28},{5,1},{9... | collective-permute-start | bytes 709640 | tf_op jit(solution)/shard_map/ppermute | solution.py:16
  33.9 0.0 collective-permute-start.6
  33.9 0.0 copy-done.2
  33.9 4.4 %collective-permute-done.7 = f32[7,22,3,128]{3,1,2,0:T(8,128)S(1)} collective-permute-done((f32[7,22,3,128]{3,1,2,0:T(8,128)S(1)}, f32[7,22,3,128]{3,1,2,0:T(8,128)S(1)}, u32[]{:S(2)}, u32[]{:S(2)}) %collective-permute-start.7) | collective-permute-done | bytes 236576 | tf_op jit(solution)/shard_map/ppermute | solution.py:16
  38.4 2.2 %collective-permute-done.6 = f32[7,22,3,128]{3,1,2,0:T(8,128)S(1)} collective-permute-done((f32[7,22,3,128]{3,1,2,0:T(8,128)S(1)}, f32[7,22,3,128]{3,1,2,0:T(8,128)S(1)}, u32[]{:S(2)}, u32[]{:S(2)}) %collective-permute-start.6) | collective-permute-done | bytes 236576 | tf_op jit(solution)/shard_map/ppermute | solution.py:13
  40.6 0.1 pad_maximum_fusion.2
  40.7 0.4 fusion.90
  41.1 1.3 %pad_maximum_fusion = f32[7,22,14,134]{3,1,2,0:T(8,128)S(1)} fusion(f32[7,22,14,3]{3,1,2,0:T(8,128)S(1)} %get-tuple-element.25, f32[7,22,3,128]{3,1,2,0:T(8,128)S(1)} %collective-permute-done.7, f32[7,3,8,128]{3,1,2,0:T(4,128)S(1)} %get-tuple-element.32, f32[7,16,8,128]{3,1,2,0:T(8,128)S(1)} %copy.51, f32[7,3,8,128]{3,1,2,0:T(4,128)S(1)} %get-tuple-element.31, ...), kind=kLoop, calls=%fused_computation | loop fusion | flops 1733424 | bytes 2311232 | tf_op jit(solution)/shard_map/concatenate | solution.py:169
  42.3 0.7 %fusion.25 = (f32[6,22,8,134]{3,1,2,0:T(8,128)S(1)}, f32[6,22,8,134]{3,1,2,0:T(8,128)S(1)}) fusion(f32[7,22,14,134]{3,1,2,0:T(8,128)S(1)} %pad_maximum_fusion), kind=kLoop, calls=%fused_computation.43 | loop fusion | flops 2688576 | bytes 5094144 | tf_op jit(solution)/shard_map/div | solution.py:41
  43.1 1.0 %fusion.7 = f32[6,16,14,134]{3,1,2,0:T(8,128)S(1)} fusion(f32[7,22,14,134]{3,1,2,0:T(8,128)S(1)} %pad_maximum_fusion), kind=kLoop, calls=%fused_computation.14 | loop fusion | flops 1981056 | bytes 5763072 | tf_op jit(solution)/shard_map/div | solution.py:41
  44.1 3.1 %pad_maximum_fusion.1 = (f32[7,22,14,131]{3,1,2,0:T(8,128)S(1)}, f32[7,22,14,131]{3,1,2,0:T(8,128)S(1)}) fusion(f32[7,22,14,3]{3,1,2,0:T(8,128)S(1)} %get-tuple-element.25, f32[7,22,3,128]{3,1,2,0:T(8,128)S(1)} %collective-permute-done.7, f32[7,3,8,128]{3,1,2,0:T(4,128)S(1)} %get-tuple-element.32, f32[7,16,8,128]{3,1,2,0:T(8,128)S(1)} %copy.51, ...), kind=kLoop, calls=%fused_computation.1 | loop fusion | flops 2824360 | bytes 3415104 | tf_op jit(solution)/shard_map/concatenate | solution.py:169
  47.2 1.4 %fusion.29 = (f32[6,22,14,128]{3,1,2,0:T(8,128)S(1)}, f32[6,22,14,128]{3,1,2,0:T(8,128)S(1)}) fusion(f32[7,22,14,128]{3,1,2,0:T(8,128)S(1)} %pad_maximum_fusion.2, f32[7,22,14,131]{3,1,2,0:T(8,128)S(1)} %get-tuple-element.24, f32[7,22,14,131]{3,1,2,0:T(8,128)S(1)} %get-tuple-element.23), kind=kLoop, calls=%fused_computation.49 | loop fusion | flops 4494336 | bytes 8515584 | tf_op jit(solution)/shard_map/div | solution.py:41
  48.6 1.6 %fusion.18 = f32[7,22,14,128]{3,1,2,0:T(8,128)S(1)} fusion(f32[7,22,14,131]{3,1,2,0:T(8,128)S(1)} %get-tuple-element.24, f32[7,22,14,131]{3,1,2,0:T(8,128)S(1)} %get-tuple-element.23), kind=kLoop, calls=%fused_computation.32 | loop fusion | flops 2207744 | bytes 7727104 | tf_op jit(solution)/shard_map/div | solution.py:32
  50.2 0.4 fusion.13
  50.6 0.9 %fusion.1 = f32[7,16,14,134]{3,1,2,0:T(8,128)S(1)} fusion(f32[7,22,14,134]{3,1,2,0:T(8,128)S(1)} %pad_maximum_fusion), kind=kLoop, calls=%fused_computation.5 | loop fusion | flops 1680896 | bytes 5883136 | tf_op jit(solution)/shard_map/div | solution.py:32
  51.5 0.4 fusion.36
  51.9 0.2 fusion.41
  52.1 0.5 fusion.31
  52.5 0.4 fusion.78
  53.0 0.3 fusion.69
  53.3 0.2 fusion.59
  53.6 0.0 copy-start
  53.6 0.0 copy-start.1
  53.6 0.1 fusion.51
  53.7 0.1 fusion.49
  53.8 0.1 subtract_dynamic-update-slice_fusion.1
  53.9 0.1 subtract_dynamic-update-slice_fusion
  54.0 0.6 %copy-done = f32[7,16,8,128]{3,2,1,0:T(8,128)S(1)} copy-done((f32[7,16,8,128]{3,2,1,0:T(8,128)S(1)}, f32[7,16,8,128]{3,2,1,0:T(8,128)}, u32[]{:S(2)}) %copy-start) | copy-done | bytes 458776
  54.6 0.1 copy-done.1
  54.7 0.2 multiply_add_fusion
  54.9 0.9 %copy.52 = f32[7,16,8,128]{3,2,1,0:T(8,128)} copy(f32[7,16,8,128]{3,1,2,0:T(8,128)S(1)} %get-tuple-element.8) | data formatting | bytes 917504
  55.9 0.9 %copy.53 = f32[7,16,8,128]{3,2,1,0:T(8,128)} copy(f32[7,16,8,128]{3,1,2,0:T(8,128)S(1)} %get-tuple-element.9) | data formatting | bytes 917504
  (7 shorter events, 0.2 us)
Async XLA Ops:
  1.8 9.1 %collective-permute-start.1 = (f32[7,3,8,128]{3,1,2,0:T(4,128)S(1)}, f32[7,3,8,128]{3,1,2,0:T(4,128)S(1)}, u32[]{:S(2)}, u32[]{:S(2)}) collective-permute-start(f32[7,3,8,128]{3,1,2,0:T(4,128)S(1)} %get-tuple-element.29), channel_id=1, source_target_pairs={{0,1},{1,2},{2,3},{3,0},{4,5},{5,6},{6,7},{7,4},{8,9},{9,10},{10,1... | collective-permute-start | bytes 258056 | tf_op jit(solution)/shard_map/ppermute | solution.py:13
  4.9 7.1 %collective-permute-start = (f32[7,3,8,128]{3,1,2,0:T(4,128)S(1)}, f32[7,3,8,128]{3,1,2,0:T(4,128)S(1)}, u32[]{:S(2)}, u32[]{:S(2)}) collective-permute-start(f32[7,3,8,128]{3,1,2,0:T(4,128)S(1)} %get-tuple-element.30), channel_id=1, source_target_pairs={{1,0},{2,1},{3,2},{0,3},{5,4},{6,5},{7,6},{4,7},{9,8},{10,9},{11,1... | collective-permute-start | bytes 258056 | tf_op jit(solution)/shard_map/ppermute | solution.py:16
  12.0 3.9 %collective-permute-start.2 = (f32[7,3,8,128]{3,1,2,0:T(4,128)S(1)}, f32[7,3,8,128]{3,1,2,0:T(4,128)S(1)}, u32[]{:S(2)}, u32[]{:S(2)}) collective-permute-start(f32[7,3,8,128]{3,1,2,0:T(4,128)S(1)} %broadcast_select_fusion.1), channel_id=1, source_target_pairs={{0,28},{4,0},{8,4},{12,8},{16,12},{20,16},{24,20},{28,24},{1,29},{... | collective-permute-start | bytes 258056 | tf_op jit(solution)/shard_map/ppermute | solution.py:23
  15.9 18.0 %copy-start.2 = (f32[3,16,8,128]{3,2,1,0:T(8,128)S(1)}, f32[3,16,8,128]{3,2,1,0:T(8,128)}, u32[]{:S(2)}) copy-start(f32[3,16,8,128]{3,2,1,0:T(8,128)} %param.6) | copy-start | bytes 589828
  15.9 5.6 %collective-permute-start.3 = (f32[7,3,8,128]{3,1,2,0:T(4,128)S(1)}, f32[7,3,8,128]{3,1,2,0:T(4,128)S(1)}, u32[]{:S(2)}, u32[]{:S(2)}) collective-permute-start(f32[7,3,8,128]{3,1,2,0:T(4,128)S(1)} %broadcast_select_fusion.2), channel_id=1, source_target_pairs={{0,24},{4,28},{8,0},{12,4},{16,8},{20,12},{24,16},{28,20},{1,25},{... | collective-permute-start | bytes 258056 | tf_op jit(solution)/shard_map/ppermute | solution.py:23
  21.5 4.9 %collective-permute-start.4 = (f32[7,3,8,128]{3,1,2,0:T(4,128)S(1)}, f32[7,3,8,128]{3,1,2,0:T(4,128)S(1)}, u32[]{:S(2)}, u32[]{:S(2)}) collective-permute-start(f32[7,3,8,128]{3,1,2,0:T(4,128)S(1)} %broadcast_select_fusion.3), channel_id=1, source_target_pairs={{0,16},{4,20},{8,24},{12,28},{16,0},{20,4},{24,8},{28,12},{1,17},{... | collective-permute-start | bytes 258056 | tf_op jit(solution)/shard_map/ppermute | solution.py:23
  26.4 4.5 %collective-permute-start.5 = (f32[7,3,8,128]{3,1,2,0:T(4,128)S(1)}, f32[7,3,8,128]{3,1,2,0:T(4,128)S(1)}, u32[]{:S(2)}, u32[]{:S(2)}) collective-permute-start(f32[7,3,8,128]{3,1,2,0:T(4,128)S(1)} %broadcast_select_fusion.4), channel_id=1, source_target_pairs={{0,28},{4,0},{8,4},{12,8},{16,12},{20,16},{24,20},{28,24},{1,29},{... | collective-permute-start | bytes 258056 | tf_op jit(solution)/shard_map/ppermute | solution.py:23
  31.1 7.3 %collective-permute-start.7 = (f32[7,22,3,128]{3,1,2,0:T(8,128)S(1)}, f32[7,22,3,128]{3,1,2,0:T(8,128)S(1)}, u32[]{:S(2)}, u32[]{:S(2)}) collective-permute-start(f32[7,22,3,128]{3,1,2,0:T(8,128)S(1)} %get-tuple-element.28), channel_id=1, source_target_pairs={{4,0},{8,4},{12,8},{16,12},{20,16},{24,20},{28,24},{0,28},{5,1},{9... | collective-permute-start | bytes 709640 | tf_op jit(solution)/shard_map/ppermute | solution.py:16
  33.9 6.7 %collective-permute-start.6 = (f32[7,22,3,128]{3,1,2,0:T(8,128)S(1)}, f32[7,22,3,128]{3,1,2,0:T(8,128)S(1)}, u32[]{:S(2)}, u32[]{:S(2)}) collective-permute-start(f32[7,22,3,128]{3,1,2,0:T(8,128)S(1)} %get-tuple-element.27), channel_id=1, source_target_pairs={{0,4},{4,8},{8,12},{12,16},{16,20},{20,24},{24,28},{28,0},{1,5},{5... | collective-permute-start | bytes 709640 | tf_op jit(solution)/shard_map/ppermute | solution.py:13
  53.6 1.0 %copy-start = (f32[7,16,8,128]{3,2,1,0:T(8,128)S(1)}, f32[7,16,8,128]{3,2,1,0:T(8,128)}, u32[]{:S(2)}) copy-start(f32[7,16,8,128]{3,2,1,0:T(8,128)} %param.4) | copy-start | bytes 1376260
  53.6 1.1 %copy-start.1 = (f32[7,16,8,128]{3,2,1,0:T(8,128)S(1)}, f32[7,16,8,128]{3,2,1,0:T(8,128)}, u32[]{:S(2)}) copy-start(f32[7,16,8,128]{3,2,1,0:T(8,128)} %param.5) | copy-start | bytes 1376260
where the time goes:
time: 57 us; the launch traced here: 56.8 us
  waiting for transfers between devices  24.3 us (43%)
  other arithmetic  13.5 us (24%)
  starting transfers between devices  13.4 us (24%)
  local copies, waits for them, and re-layouts  4.11 us (7%)
  between operations  1.53 us (3%)
    ppermute x4, waiting for transfers between devices, passed_along(): lax.ppermute(value, axis, [(i, (i + by) % peers) for i in range(peers)])  12.7 us
    ppermute x2, waiting for transfers between devices, padded_2(): lax.ppermute(lax.slice_in_dim(block, block.shape[dim] - width, None, axis...  6.09 us
    ppermute x2, waiting for transfers between devices, padded_2(): lax.ppermute(lax.slice_in_dim(block, 0, width, axis=dim), axis, backward)  5.49 us
    ppermute x4, starting transfers between devices, passed_along(): lax.ppermute(value, axis, [(i, (i + by) % peers) for i in range(peers)])  5.41 us
    ppermute x2, starting transfers between devices, padded_2(): lax.ppermute(lax.slice_in_dim(block, 0, width, axis=dim), axis, backward)  4.89 us
    concatenate x2, other arithmetic, per_device(): jnp.concatenate([padded[:, :, :, -3:], padded, padded[:, :, :, :3]], axis=3)  4.31 us
    div x6, other arithmetic, first_diff(): (45.0 * (part(1) - part(-1)) - 9.0 * (part(2) - part(-2)) + (part(3) - pa...  3.94 us
    unnamed x9, local copies, waits for them, and re-layouts  3.67 us
  transfers between devices with their start and end apart: 8, of which 8 were waited for; matrix products, arithmetic and copies ran while one was open for 0% of the time, Pallas kernels for 0%

commit v1 on v0

v1 whole, which is shorter than its diff:
```python
import functools

import jax
import jax.numpy as jnp
import numpy as np
from jax import lax
from jax.experimental import pallas as pl
from jax.experimental.pallas import tpu as pltpu
from jax.sharding import PartitionSpec as P

LANES = 128
FIRST = ((1, 45.0), (2, -9.0), (3, 1.0))
SECOND = ((1, 270.0), (2, -27.0), (3, 2.0))
MIXED = (0, 1, 3, 4)
PLAIN = (2, 5, 6)
SHEAR_Z = (1, 2, 4, 5)
ROW = 8
TALL = 24
VMEM = 32 * 1024 * 1024


def z_weights():
    one = np.zeros((LANES, 2 * LANES), np.float32)
    cells = np.arange(LANES)
    one[cells, LANES + cells] = -490.0
    for step, weight in FIRST:
        one[(cells + step) % LANES, cells] += weight
        one[(cells - step) % LANES, cells] -= weight
    for step, weight in SECOND:
        one[(cells + step) % LANES, LANES + cells] += weight
        one[(cells - step) % LANES, LANES + cells] += weight
    return np.concatenate([one, one]).astype(jnp.bfloat16)


def along_z(value, weights):
    upper = value.astype(jnp.bfloat16)
    rest = (value - upper.astype(jnp.float32)).astype(jnp.bfloat16)
    return jnp.dot(
        jnp.concatenate([upper, rest], axis=1), weights, preferred_element_type=jnp.float32
    )


def first_diff(part):
    return (
        0.75 * (part(1) - part(-1))
        - 0.15 * (part(2) - part(-2))
        + (1.0 / 60.0) * (part(3) - part(-3))
    )


def second_diff(part):
    return (
        (-490.0 / 180.0) * part(0)
        + 1.5 * (part(1) + part(-1))
        - 0.15 * (part(2) + part(-2))
        + (1.0 / 90.0) * (part(3) + part(-3))
    )


def x_terms(planes_of, mixes_of):
    grad = [first_diff(planes_of(field)) for field in range(7)]
    mix = [first_diff(mixes_of(number)) for number in range(6)]
    viscous = (
        (4.0 / 3.0) * second_diff(planes_of(0)) + (1.0 / 3.0) * mix[0],
        second_diff(planes_of(1)) + (1.0 / 3.0) * mix[1],
        second_diff(planes_of(2)) + (1.0 / 3.0) * mix[2],
    )
    current = (
        mix[3],
        mix[4] - second_diff(planes_of(4)),
        mix[5] - second_diff(planes_of(5)),
    )
    return grad, viscous, current


def rates_of(center, force, index, inv_width, grads, viscous, curr):
    velx, vely, velz, potx, poty, potz, logr = center
    grad_x, grad_y, grad_z = grads
    field_x = grad_y[5] - grad_z[4]
    field_y = grad_z[3] - grad_x[5]
    field_z = grad_x[4] - grad_y[3] + 0.5
    lorentz = (
        curr[1] * field_z - curr[2] * field_y,
        curr[2] * field_x - curr[0] * field_z,
        curr[0] * field_y - curr[1] * field_x,
    )
    emf = (
        vely * field_z - velz * field_y,
        velz * field_x - velx * field_z,
        velx * field_y - vely * field_x,
    )
    inv_rho = jnp.exp(-logr)
    flow = -1.5 * ((index.astype(jnp.float32) + 0.5) * inv_width - 0.5)
    shear_rate = -1.5 * inv_width
    carried = vely + flow
    divu = grad_x[0] + grad_y[1] + grad_z[2]

    def advect(comp):
        return velx * grad_x[comp] + carried * grad_y[comp] + velz * grad_z[comp]

    rates = []
    for comp in range(3):
        total = (-2.0 / 3.0) * divu * grads[comp][6]
        for col in range(3):
            total = total + (grads[col][comp] + grads[comp][col]) * grads[col][6]
        rate = lorentz[comp] * inv_rho - advect(comp) - grads[comp][6] + force[comp]
        rate = rate + 0.05 * (viscous[comp] + total)
        if comp == 0:
            rate = rate + vely
        if comp == 1:
            rate = rate - (1.0 + shear_rate) * velx
        rates.append(rate)
    for comp in range(3):
        rate = emf[comp] - flow * grad_y[3 + comp] - 0.05 * curr[comp]
        if comp == 0:
            rate = rate - shear_rate * poty
        rates.append(rate)
    rates.append(-advect(6) - divu)
    return rates


def pack_kernel(cells_x, cells_y, state, held, y_near, y_far, x_near, x_far, sems):
    copies = [
        pltpu.make_async_copy(state.at[field], held.at[field], sems.at[field]) for field in range(7)
    ]
    for copy in copies:
        copy.start()
    y_odd = lax.axis_index("yz") % 2
    x_odd = lax.axis_index("gx") % 2
    for field, copy in enumerate(copies):
        copy.wait()

        def rows(first, then):
            for plane in range(cells_x):
                at = 3 * (field * cells_x + plane)
                first[at : at + 3] = held[field, plane, cells_y - 3 :]
                then[at : at + 3] = held[field, plane, :3]

        def planes(first, then):
            first[field] = held[field, cells_x - 3 :]
            then[field] = held[field, :3]

        pl.when(y_odd == 0)(functools.partial(rows, y_near, y_far))
        pl.when(y_odd == 1)(functools.partial(rows, y_far, y_near))
        pl.when(x_odd == 0)(functools.partial(planes, x_near, x_far))
        pl.when(x_odd == 1)(functools.partial(planes, x_far, x_near))


def side_kernel(
    cells_x, state, weights, y_near, y_far, dz, mixes, side_terms, block, z_block, dzz
):
    own = slice(ROW, ROW + 8)
    y_odd = lax.axis_index("yz") % 2
    for field in range(7):
        got = along_z(state[field].reshape(cells_x * 8, LANES), weights[...])
        dz[field] = (got[:, :LANES] * (1.0 / 60.0)).reshape(cells_x, 8, LANES)
        if field < 5:
            dzz[field] = (got[:, LANES:] * (1.0 / 180.0)).reshape(cells_x, 8, LANES)
        block[field, :, own] = state[field]
    for number, field in enumerate(SHEAR_Z):
        z_block[number, :, own] = dz[field]

    def ghosts(target, rows):
        for field in range(7):
            for plane in range(cells_x):
                at = 3 * (field * cells_x + plane)
                block[field, plane, target : target + 3] = rows[at : at + 3]
        got = along_z(rows[...], weights[:, :LANES]) * (1.0 / 60.0)
        for number, field in enumerate(SHEAR_Z):
            for plane in range(cells_x):
                at = 3 * (field * cells_x + plane)
                z_block[number, plane, target : target + 3] = got[at : at + 3]

    @pl.when(y_odd == 0)
    def _():
        ghosts(ROW + 8, y_near)
        ghosts(ROW - 3, y_far)

    @pl.when(y_odd == 1)
    def _():
        ghosts(ROW - 3, y_near)
        ghosts(ROW + 8, y_far)

    def yz_step(plane, carry):
        def rows_of(field):
            return lambda step: block[field, plane, ROW + step : ROW + 8 + step]

        def z_rows_of(number):
            return lambda step: z_block[number, plane, ROW + step : ROW + 8 + step]

        grad = [first_diff(rows_of(field)) for field in range(7)]
        cross = [first_diff(z_rows_of(number)) for number in range(4)]
        terms = grad + [
            second_diff(rows_of(0)) + dzz[0, plane],
            (4.0 / 3.0) * second_diff(rows_of(1)) + dzz[1, plane] + (1.0 / 3.0) * cross[1],
            second_diff(rows_of(2)) + (4.0 / 3.0) * dzz[2, plane] + (1.0 / 3.0) * cross[0],
            -(second_diff(rows_of(3)) + dzz[3, plane]),
            cross[3] - dzz[4, plane],
            cross[2] - second_diff(rows_of(5)),
        ]
        for number, term in enumerate(terms):
            side_terms[number, plane] = term
        mixes[0, plane] = grad[1] + dz[2, plane]
        mixes[1, plane] = grad[0]
        mixes[2, plane] = dz[0, plane]
        mixes[3, plane] = grad[4] + dz[5, plane]
        mixes[4, plane] = grad[3]
        mixes[5, plane] = dz[3, plane]
        return carry

    lax.fori_loop(0, cells_x, yz_step, 0)


def corner_kernel(slabs_x, x_near, x_far, after, faces, to_next, to_last):
    where_x = lax.axis_index("gx")
    x_odd = where_x % 2

    def order(low, high):
        faces[0] = low[...]
        faces[1] = high[...]

    pl.when(x_odd == 0)(functools.partial(order, x_far, x_near))
    pl.when(x_odd == 1)(functools.partial(order, x_near, x_far))
    for side in range(2):
        for number, field in enumerate(MIXED):
            for plane in range(3):
                at = 3 * (3 * (4 * side + number) + plane)
                to_next[at : at + 3] = faces[side, field, plane, 5:8]
                to_last[at : at + 3] = faces[side, field, plane, 0:3]

    def fill(side):
        for number, field in enumerate(MIXED + PLAIN):
            for plane in range(3):
                at = 72 + 4 * (3 * number + plane)
                row = 1 if field in MIXED else 4
                to_next[at : at + 4] = faces[side, field, plane, row : row + 4]
                row = 3 if field in MIXED else 0
                to_last[at : at + 4] = faces[side, field, plane, row : row + 4]

    pl.when(where_x == 0)(functools.partial(fill, 0))
    pl.when(where_x == slabs_x - 1)(functools.partial(fill, 1))


def finish(inv_width, index, center, force, old, x_parts, side, grad_z):
    grad_x, viscous, curr = x_parts
    rates = rates_of(
        center,
        force,
        index,
        inv_width,
        (grad_x, side[:7], grad_z),
        [viscous[comp] + side[7 + comp] for comp in range(3)],
        [curr[comp] + side[10 + comp] for comp in range(3)],
    )
    fresh = [(-5.0 / 9.0) * old[field] + 0.15 * rates[field] for field in range(7)]
    return [center[field] + (15.0 / 16.0) * fresh[field] for field in range(7)], fresh


def inner_kernel(
    cells_x, inv_width,
    state, register, forcing, dz, mixes, side_terms,
    new_state, new_register,
    fresh_state, fresh_register, sems,
):
    first = lax.axis_index("gx") * cells_x

    def plane_step(plane, carry):
        states, registers = finish(
            inv_width,
            first + plane,
            [state[field, plane] for field in range(7)],
            [forcing[comp, plane] for comp in range(3)],
            [register[field, plane] for field in range(7)],
            x_terms(
                lambda field: lambda step: state[field, plane + step],
                lambda number: lambda step: mixes[number, plane + step],
            ),
            [side_terms[number, plane] for number in range(13)],
            [dz[field, plane] for field in range(7)],
        )
        for field in range(7):
            fresh_register[field, plane] = registers[field]
            fresh_state[field, plane] = states[field]
        return carry

    middle = cells_x // 2
    copies = []
    for number, (begin, end) in enumerate(((3, middle), (middle, cells_x - 3))):
        lax.fori_loop(begin, end, plane_step, 0)
        for which, (fresh, final) in enumerate(((fresh_state, new_state), (fresh_register, new_register))):
            copy = pltpu.make_async_copy(
                fresh.at[:, pl.ds(begin, end - begin)],
                final.at[:, pl.ds(begin, end - begin)],
                sems.at[2 * number + which],
            )
            copy.start()
            copies.append(copy)
    for copy in copies:
        copy.wait()


def edge_kernel(
    cells_x, slabs_x, slabs_y, cells_y, inv_width,
    y_shift, state, register, forcing, weights, dz, mixes, side_terms,
    planes, from_last, from_next, kept_state, kept_register,
    new_state, new_register,
    ghost, faces, face_mixes, fresh_state, fresh_register, sems,
):
    where_x = lax.axis_index("gx")
    first = where_x * cells_x
    lean = (y_shift[0] + cells_y // 2) % cells_y - cells_y // 2
    at_low, at_high = where_x == 0, where_x == slabs_x - 1
    for side in range(2):
        for number, field in enumerate(MIXED):
            for plane in range(3):
                at = 3 * (3 * (4 * side + number) + plane)
                ghost[side, field, plane, 13:16] = from_last[at : at + 3]
                ghost[side, field, plane, 24:27] = from_next[at : at + 3]
        for field in range(7):
            for plane in range(3):
                ghost[side, field, plane, 16:24] = planes[side, field, plane]

    def put(side):
        for number, field in enumerate(MIXED + PLAIN):
            for plane in range(3):
                at = 72 + 4 * (3 * number + plane)
                row = 9 if field in MIXED else 12
                ghost[side, field, plane, row : row + 4] = from_last[at : at + 4]
                row = 27 if field in MIXED else 24
                ghost[side, field, plane, row : row + 4] = from_next[at : at + 4]

    pl.when(at_low)(functools.partial(put, 0))
    pl.when(at_high)(functools.partial(put, 1))
    for side, shift in enumerate((jnp.where(at_low, lean, 0), jnp.where(at_high, -lean, 0))):
        shift = shift + 16
        for field in range(7):
            for plane in range(3):
                faces[side, field, plane] = ghost[side, field, plane, pl.ds(shift, 8)]
        got = along_z(
            jnp.concatenate([faces[side, field].reshape(24, LANES) for field in (0, 2, 3, 5)]),
            weights[:, :LANES],
        ) * (1.0 / 60.0)
        for plane in range(3):
            def rows_of(field):
                return lambda step: ghost[side, field, plane, pl.ds(shift + step, 8)]

            def depth(number):
                return got[24 * number + 8 * plane : 24 * number + 8 * plane + 8]

            face_mixes[side, 0, plane] = first_diff(rows_of(1)) + depth(1)
            face_mixes[side, 1, plane] = first_diff(rows_of(0))
            face_mixes[side, 2, plane] = depth(0)
            face_mixes[side, 3, plane] = first_diff(rows_of(4)) + depth(3)
            face_mixes[side, 4, plane] = first_diff(rows_of(3))
            face_mixes[side, 5, plane] = depth(2)

    copies = []
    for side in range(2):
        begin = side * (cells_x - 3)
        for local in range(3):
            plane = begin + local

            def at(own, far, number, step):
                spot = plane + step
                if spot < 0:
                    return far[0, number, spot + 3]
                if spot >= cells_x:
                    return far[1, number, spot - cells_x]
                return own[number, spot]

            states, registers = finish(
                inv_width,
                first + plane,
                [state[field, plane] for field in range(7)],
                [forcing[comp, plane] for comp in range(3)],
                [register[field, plane] for field in range(7)],
                x_terms(
                    lambda field: lambda step: at(state, faces, field, step),
                    lambda number: lambda step: at(mixes, face_mixes, number, step),
                ),
                [side_terms[number, plane] for number in range(13)],
                [dz[field, plane] for field in range(7)],
            )
            for field in range(7):
                fresh_register[side, field, local] = registers[field]
                fresh_state[side, field, local] = states[field]
        for which, (fresh, final) in enumerate(((fresh_state, new_state), (fresh_register, new_register))):
            copy = pltpu.make_async_copy(
                fresh.at[side], final.at[:, pl.ds(begin, 3)], sems.at[2 * side + which]
            )
            copy.start()
            copies.append(copy)
    for copy in copies:
        copy.wait()


def per_device(slabs_x, slabs_y, state, register, forcing, y_shift):
    cells_x, cells_y = state.shape[1], state.shape[2]
    total_x, total_y = cells_x * slabs_x, cells_y * slabs_y
    steps = (y_shift[0] + cells_y // 2) // cells_y

    def shape(*dims):
        return jax.ShapeDtypeStruct(dims, jnp.float32)

    smem = pl.BlockSpec(memory_space=pltpu.SMEM)
    vmem = pl.BlockSpec(memory_space=pltpu.VMEM)
    anyspace = pl.BlockSpec(memory_space=pl.ANY)
    params = pltpu.CompilerParams(vmem_limit_bytes=VMEM)
    weights = jnp.asarray(z_weights())

    held, y_near, y_far, x_near, x_far = pl.pallas_call(
        functools.partial(pack_kernel, cells_x, cells_y),
        out_shape=[
            shape(*state.shape),
            shape(21 * cells_x, LANES), shape(21 * cells_x, LANES),
            shape(7, 3, cells_y, LANES), shape(7, 3, cells_y, LANES),
        ],
        in_specs=[anyspace],
        out_specs=[vmem] * 5,
        scratch_shapes=[pltpu.SemaphoreType.DMA((7,))],
        compiler_params=params,
    )(state)

    digit = min(slabs_y, 8)

    def place(slab, along):
        return along % slabs_y * slabs_x + slab

    def send(value, pairs):
        return lax.ppermute(value, ("yz", "gx"), pairs)

    def both(pairs):
        return pairs + [(b, a) for a, b in pairs]

    def y_pairs(odd):
        return both(
            [(place(slab, j), place(slab, j + 1)) for slab in range(slabs_x) for j in range(odd, slabs_y, 2)]
        )

    def x_pairs(odd, by):
        return both(
            [
                (place(slab, j + by * (slab == slabs_x - 1)), place((slab + 1) % slabs_x, j))
                for slab in range(odd, slabs_x, 2)
                for j in range(slabs_y)
            ]
        )

    if slabs_y > digit:
        where_x = lax.axis_index("gx")
        at_low, at_high = where_x == 0, where_x == slabs_x - 1
        groups = steps // digit
        amount = jnp.where(at_high, groups, slabs_y // digit - groups) % (slabs_y // digit)
        across = x_far
        hop = 1
        while hop < slabs_y // digit:
            pairs = [(i, (i - hop * digit) % slabs_y) for i in range(slabs_y)]
            moved = lax.ppermute(across, "yz", pairs)
            across = jnp.where((amount // hop) % 2 == 1, moved, across)
            hop *= 2
        x_far = jnp.where(at_low | at_high, across, x_far)

    def exchange(by, operands):
        y_near, y_far, x_near, x_far, state, weights = operands
        y_near = send(y_near, y_pairs(0))
        x_near = send(x_near, x_pairs(0, 0))
        x_far = send(x_far, x_pairs(1, by))
        y_far = send(y_far, y_pairs(1))
        terms = pl.pallas_call(
            functools.partial(side_kernel, cells_x),
            out_shape=[shape(*state.shape), shape(6, *state.shape[1:]), shape(13, *state.shape[1:])],
            in_specs=[vmem] * 4,
            out_specs=[vmem] * 3,
            scratch_shapes=[
                pltpu.VMEM((7, cells_x, TALL, LANES), jnp.float32),
                pltpu.VMEM((4, cells_x, TALL, LANES), jnp.float32),
                pltpu.VMEM((5, *state.shape[1:]), jnp.float32),
            ],
            compiler_params=params,
            cost_estimate=pl.CostEstimate(flops=2 * 10**8, bytes_accessed=10**6, transcendentals=0),
        )(state, weights, y_near, y_far)
        corners = pl.pallas_call(
            functools.partial(corner_kernel, slabs_x),
            out_shape=[shape(2, *x_near.shape), shape(160, LANES), shape(160, LANES)],
            in_specs=[vmem] * 2 + [anyspace],
            out_specs=[vmem] * 3,
            compiler_params=params,
        )(x_near, x_far, terms[2])
        return (*terms, *corners)

    dz, mixes, side_terms, faces, to_next, to_last = lax.switch(
        steps % digit,
        [functools.partial(exchange, by) for by in range(digit)],
        (y_near, y_far, x_near, x_far, held, weights),
    )
    beside = [
        [(place(slab, j), place(slab, j + along)) for slab in range(slabs_x) for j in range(slabs_y)]
        for along in (1, -1)
    ]
    from_last = send(to_next, beside[0])
    from_next = send(to_last, beside[1])

    new_state, new_register = pl.pallas_call(
        functools.partial(inner_kernel, cells_x, 1.0 / total_x),
        out_shape=[shape(*state.shape)] * 2,
        in_specs=[vmem] * 6,
        out_specs=[anyspace] * 2,
        scratch_shapes=[
            pltpu.VMEM(state.shape, jnp.float32),
            pltpu.VMEM(state.shape, jnp.float32),
            pltpu.SemaphoreType.DMA((4,)),
        ],
        compiler_params=params,
        cost_estimate=pl.CostEstimate(flops=2 * 10**8, bytes_accessed=2 * 10**6, transcendentals=0),
    )(held, register, forcing, dz, mixes, side_terms)

    return pl.pallas_call(
        functools.partial(edge_kernel, cells_x, slabs_x, slabs_y, cells_y, 1.0 / total_x),
        out_shape=[shape(*state.shape)] * 2,
        in_specs=[smem] + [vmem] * 10 + [anyspace] * 2,
        out_specs=[anyspace] * 2,
        input_output_aliases={11: 0, 12: 1},
        scratch_shapes=[
            pltpu.VMEM((2, 7, 3, 40, LANES), jnp.float32),
            pltpu.VMEM((2, 7, 3, 8, LANES), jnp.float32),
            pltpu.VMEM((2, 6, 3, 8, LANES), jnp.float32),
            pltpu.VMEM((2, 7, 3, 8, LANES), jnp.float32),
            pltpu.VMEM((2, 7, 3, 8, LANES), jnp.float32),
            pltpu.SemaphoreType.DMA((4,)),
        ],
        compiler_params=params,
    )(
        y_shift, held, register, forcing, weights, dz, mixes, side_terms,
        faces, from_last, from_next, new_state, new_register,
    )


def solution(mesh):
    spec = P(None, "gx", "yz", None)
    return jax.shard_map(
        functools.partial(per_device, mesh.shape["gx"], mesh.shape["yz"]),
        mesh=mesh,
        in_specs=(spec, spec, spec, P()),
        out_specs=(spec, spec),
        check_vma=False,
    )
```

time: 57 us -> 24.7 us (0.43)
  waiting for transfers between devices: 24.3 us -> 3.96 us
  other arithmetic: 13.5 us -> 0 us
  Pallas kernels: 0 us -> 7.87 us
  starting transfers between devices: 13.4 us -> 10.1 us
  local copies, waits for them, and re-layouts: 4.11 us -> 1.11 us
    ppermute x8 -> x6, waiting for transfers between devices: 24.3 us -> 3.96 us  [send(): return lax.ppermute(value, ('yz', 'gx'), pairs)]
    pallas_call x0 -> x5, Pallas kernels: none -> 7.87 us  [the longest x1 2.39 us: per_device(): pl.pallas_call(functools.partial(inner_kernel, cells_x, 1.0 / total_x), o...]
    div x9 -> x0, other arithmetic: 7.09 us -> none  [the longest x6 3.94 us: first_diff(): (45.0 * (part(1) - part(-1)) - 9.0 * (part(2) - part(-2)) + (part(3) - pa...]
    concatenate x3 -> x0, other arithmetic: 4.44 us -> none  [the longest x2 4.31 us: per_device(): jnp.concatenate([padded[:, :, :, -3:], padded, padded[:, :, :, :3]], axis=3)]
    ppermute x8 -> x6, starting transfers between devices: 13.4 us -> 10.1 us  [send(): return lax.ppermute(value, ('yz', 'gx'), pairs)]
    unnamed x9 -> x8, local copies, waits for them, and re-layouts: 3.67 us -> 1.11 us
    unnamed x6 -> x0, other arithmetic: 1.27 us -> none
  transfers between devices with their start and end apart: 8 -> 6, of which waited for: 8 -> 3; matrix products, arithmetic and copies ran while one was open for 0% -> 0% of each run, Pallas kernels for 0% -> 19%
where the time goes in v1:
time: 24.7 us; the launch traced here: 24.4 us
  starting transfers between devices  10.1 us (41%)
  Pallas kernels  7.87 us (32%)
  waiting for transfers between devices  3.96 us (16%)
  between operations  1.36 us (6%)
  local copies, waits for them, and re-layouts  1.11 us (4%)
    ppermute x6, starting transfers between devices, send(): return lax.ppermute(value, ('yz', 'gx'), pairs)  10.1 us
    ppermute x6, waiting for transfers between devices, send(): return lax.ppermute(value, ('yz', 'gx'), pairs)  3.96 us
    pallas_call x1, Pallas kernels, per_device(): pl.pallas_call(functools.partial(inner_kernel, cells_x, 1.0 / total_x), o...  2.39 us
    pallas_call x1, Pallas kernels, exchange(): pl.pallas_call(functools.partial(side_kernel, cells_x), out_shape=[shape(...  2.32 us
    pallas_call x1, Pallas kernels, per_device(): pl.pallas_call(functools.partial(edge_kernel, cells_x, slabs_x, slabs_y,...  2.3 us
    unnamed x8, local copies, waits for them, and re-layouts  1.11 us
    pallas_call x1, Pallas kernels, per_device(): pl.pallas_call(functools.partial(pack_kernel, cells_x, cells_y), out_shap...  0.8 us
  transfers between devices with their start and end apart: 6, of which 3 were waited for; matrix products, arithmetic and copies ran while one was open for 0% of the time, Pallas kernels for 19%

profile of v1, /device:TPU:0, one launch (start us, length us, event | category | flops | bytes accessed | tf_op | source)
XLA Modules:
  0.0 24.4 jit_solution(18010055186716900941)
XLA Ops:
  1.3 0.0 copy-start.2
  1.3 1.0 %copy-done.2 = f32[7,16,8,128]{3,2,1,0:T(8,128)S(1)} copy-done((f32[7,16,8,128]{3,2,1,0:T(8,128)S(1)}, f32[7,16,8,128]{3,2,1,0:T(8,128)}, u32[]{:S(2)}) %copy-start.2) | copy-done | bytes 458776
  2.3 0.0 copy-start.3
  2.3 0.8 %shard_map.68 = (f32[7,16,8,128]{3,2,1,0:T(8,128)S(1)}, f32[336,128]{1,0:T(8,128)S(1)}, f32[336,128]{1,0:T(8,128)S(1)}, f32[7,3,8,128]{3,2,1,0:T(8,128)S(1)}, f32[7,3,8,128]{3,2,1,0:T(8,128)S(1)}) custom-call(f32[7,16,8,128]{3,2,1,0:T(8,128)S(1)} %copy-done.2), custom_call_target="tpu_custom_call" | custom-call | tf_op jit(solution)/shard_map/pallas_call | solution.py:411
  3.1 0.1 copy-done.3
  3.2 0.0 copy-start
  3.2 0.0 copy-start.1
  3.2 13.2 %conditional.1 = (f32[7,16,8,128]{3,2,1,0:T(8,128)S(1)}, f32[6,16,8,128]{3,2,1,0:T(8,128)S(1)}, f32[13,16,8,128]{3,2,1,0:T(8,128)}, f32[2,7,3,8,128]{4,3,2,1,0:T...) conditional(s32[]{:T(128)} %clamp.3, (f32[336,128]{1,0:T(8,128)S(1)}, ...), branch_computations={%region_0.1_spmd, %region_1.2_spmd, %region_2.3_spmd, %region_3.4_... | conditional | flops 200000000 | bytes 3064592 | solution.py:491
  3.2 0.5 %collective-permute-start.28 = (f32[336,128]{1,0:T(8,128)S(1)}, f32[336,128]{1,0:T(8,128)S(1)}, u32[]{:S(2)}, u32[]{:S(2)}) collective-permute-start(f32[336,128]{1,0:T(8,128)S(1)} %get-tuple-element.182), channel_id=1, source_target_pairs={{0,4},{8,12},{16,20},{24,28},{1,5},{9,13},{17,21},{25,29},{2,6},{1... | collective-permute-start | bytes 516104 | tf_op jit(solution)/shard_map/cond/branch_7_fun/ppermute | solution.py:430
  3.7 3.6 %collective-permute-start.29 = (f32[336,128]{1,0:T(8,128)S(1)}, f32[336,128]{1,0:T(8,128)S(1)}, u32[]{:S(2)}, u32[]{:S(2)}) collective-permute-start(f32[336,128]{1,0:T(8,128)S(1)} %get-tuple-element.183), channel_id=1, source_target_pairs={{4,8},{12,16},{20,24},{28,0},{5,9},{13,17},{21,25},{29,1},{6,10},{... | collective-permute-start | bytes 516104 | tf_op jit(solution)/shard_map/cond/branch_7_fun/ppermute | solution.py:430
  7.3 1.6 %collective-permute-start.30 = (f32[7,3,8,128]{3,2,1,0:T(8,128)S(1)}, f32[7,3,8,128]{3,2,1,0:T(8,128)S(1)}, u32[]{:S(2)}, u32[]{:S(2)}) collective-permute-start(f32[7,3,8,128]{3,2,1,0:T(8,128)S(1)} %get-tuple-element.187), channel_id=1, source_target_pairs={{0,1},{4,5},{8,9},{12,13},{16,17},{20,21},{24,25},{28,29},{2,3},{6... | collective-permute-start | bytes 258056 | tf_op jit(solution)/shard_map/cond/branch_7_fun/ppermute | solution.py:430
  8.9 1.8 %collective-permute-start.31 = (f32[7,3,8,128]{3,2,1,0:T(8,128)S(1)}, f32[7,3,8,128]{3,2,1,0:T(8,128)S(1)}, u32[]{:S(2)}, u32[]{:S(2)}) collective-permute-start(f32[7,3,8,128]{3,2,1,0:T(8,128)S(1)} %get-tuple-element.188), channel_id=1, source_target_pairs={{1,2},{5,6},{9,10},{13,14},{17,18},{21,22},{25,26},{29,30},{31,0},... | collective-permute-start | bytes 258056 | tf_op jit(solution)/shard_map/cond/branch_7_fun/ppermute | solution.py:430
  10.7 0.0 collective-permute-done.28.y_near
  10.7 0.8 %collective-permute-done.29.y_far = f32[336,128]{1,0:T(8,128)S(1)} collective-permute-done((f32[336,128]{1,0:T(8,128)S(1)}, f32[336,128]{1,0:T(8,128)S(1)}, u32[]{:S(2)}, u32[]{:S(2)}) %collective-permute-start.29) | collective-permute-done | bytes 172064 | tf_op jit(solution)/shard_map/cond/branch_7_fun/ppermute | solution.py:430
  11.4 2.3 %branch_7_fun.2 = (f32[7,16,8,128]{3,2,1,0:T(8,128)S(1)}, f32[6,16,8,128]{3,2,1,0:T(8,128)S(1)}, f32[13,16,8,128]{3,2,1,0:T(8,128)}) custom-call(f32[7,16,8,128]{3,2,1,0:T(8,128)S(1)} %get-tuple-element.180.state, bf16[256,256]{1,0:T(8,128)(2,1)S(1)} %get-tuple-element.181.weights, f32[336,128]{1,0:T(8,128)S(1)} %collective-permute-done.28.y_near, ...), custom_call_target="tpu_custom_call" | custom-call | flops 200000000 | bytes 1000000 | tf_op jit(solution)/shard_map/cond/branch_7_fun/pallas_call | solution.py:469
  13.8 0.0 collective-permute-done.30.x_near
  13.8 2.6 %collective-permute-done.31.x_far = f32[7,3,8,128]{3,2,1,0:T(8,128)S(1)} collective-permute-done((f32[7,3,8,128]{3,2,1,0:T(8,128)S(1)}, f32[7,3,8,128]{3,2,1,0:T(8,128)S(1)}, u32[]{:S(2)}, u32[]{:S(2)}) %collective-permute-start.31) | collective-permute-done | bytes 86048 | tf_op jit(solution)/shard_map/cond/branch_7_fun/ppermute | solution.py:430
  16.4 0.1 branch_7_fun.3
  16.4 0.1 collective-permute-start.32
  16.5 2.6 %collective-permute-start.33 = (f32[160,128]{1,0:T(8,128)S(1)}, f32[160,128]{1,0:T(8,128)S(1)}, u32[]{:S(2)}, u32[]{:S(2)}) collective-permute-start(f32[160,128]{1,0:T(8,128)S(1)} %get-tuple-element.217), channel_id=1, source_target_pairs={{0,28},{4,0},{8,4},{12,8},{16,12},{20,16},{24,20},{28,24},{1,29},{... | collective-permute-start | bytes 245768 | tf_op jit(solution)/shard_map/ppermute | solution.py:430
  19.1 0.0 copy-done
  19.1 0.0 copy-done.1
  19.2 2.4 %shard_map.69 = (f32[7,16,8,128]{3,2,1,0:T(8,128)}, f32[7,16,8,128]{3,2,1,0:T(8,128)}) custom-call(f32[7,16,8,128]{3,2,1,0:T(8,128)S(1)} %get-tuple-element.207.state, f32[7,16,8,128]{3,2,1,0:T(8,128)S(1)} %copy-done, f32[3,16,8,128]{3,2,1,0:T(8,128)S(1)} %copy-done.1, f32[7,16,8,128]{3,2,1,0:T(8,128)S(1)} %get-tuple-element.212.dz, ...), custom_call_target="tpu_custom_call" | custom-call | flops 200000000 | bytes 2000000 | tf_op jit(solution)/shard_map/pallas_call | solution.py:503
  21.6 0.6 %collective-permute-done.32.from_last = f32[160,128]{1,0:T(8,128)S(1)} collective-permute-done((f32[160,128]{1,0:T(8,128)S(1)}, f32[160,128]{1,0:T(8,128)S(1)}, u32[]{:S(2)}, u32[]{:S(2)}) %collective-permute-start.32) | collective-permute-done | bytes 81952 | tf_op jit(solution)/shard_map/ppermute | solution.py:430
  22.1 0.0 collective-permute-done.33.from_next
  22.1 2.3 %shard_map.70 = (f32[7,16,8,128]{3,2,1,0:T(8,128)}, f32[7,16,8,128]{3,2,1,0:T(8,128)}) custom-call(s32[1]{0:T(128)S(6)} %copy.59.y_shift, f32[7,16,8,128]{3,2,1,0:T(8,128)S(1)} %get-tuple-element.207.state, f32[7,16,8,128]{3,2,1,0:T(8,128)S(1)} %copy-done, f32[3,16,8,128]{3,2,1,0:T(8,128)S(1)} %copy-done.1, ...), custom_call_target="tpu_custom_call", output_to_operand_aliasing={{0}: (11, {}), {1}: (12, {})} | custom-call | tf_op jit(solution)/shard_map/pallas_call | solution.py:517
Async XLA Ops:
  1.3 1.0 %copy-start.2 = (f32[7,16,8,128]{3,2,1,0:T(8,128)S(1)}, f32[7,16,8,128]{3,2,1,0:T(8,128)}, u32[]{:S(2)}) copy-start(f32[7,16,8,128]{3,2,1,0:T(8,128)} %state.1) | copy-start | bytes 1376260
  2.3 0.9 %copy-start.3 = (bf16[256,256]{1,0:T(8,128)(2,1)S(1)}, bf16[256,256]{1,0:T(8,128)(2,1)}, u32[]{:S(2)}) copy-start(bf16[256,256]{1,0:T(8,128)(2,1)} %constant.33.clone.weights) | copy-start | bytes 393220
  3.2 15.9 %copy-start = (f32[7,16,8,128]{3,2,1,0:T(8,128)S(1)}, f32[7,16,8,128]{3,2,1,0:T(8,128)}, u32[]{:S(2)}) copy-start(f32[7,16,8,128]{3,2,1,0:T(8,128)} %register.3) | copy-start | bytes 1376260
  3.2 15.9 %copy-start.1 = (f32[3,16,8,128]{3,2,1,0:T(8,128)S(1)}, f32[3,16,8,128]{3,2,1,0:T(8,128)}, u32[]{:S(2)}) copy-start(f32[3,16,8,128]{3,2,1,0:T(8,128)} %forcing.3) | copy-start | bytes 589828
  3.2 7.4 %collective-permute-start.28 = (f32[336,128]{1,0:T(8,128)S(1)}, f32[336,128]{1,0:T(8,128)S(1)}, u32[]{:S(2)}, u32[]{:S(2)}) collective-permute-start(f32[336,128]{1,0:T(8,128)S(1)} %get-tuple-element.182), channel_id=1, source_target_pairs={{0,4},{8,12},{16,20},{24,28},{1,5},{9,13},{17,21},{25,29},{2,6},{1... | collective-permute-start | bytes 516104 | tf_op jit(solution)/shard_map/cond/branch_7_fun/ppermute | solution.py:430
  3.7 7.7 %collective-permute-start.29 = (f32[336,128]{1,0:T(8,128)S(1)}, f32[336,128]{1,0:T(8,128)S(1)}, u32[]{:S(2)}, u32[]{:S(2)}) collective-permute-start(f32[336,128]{1,0:T(8,128)S(1)} %get-tuple-element.183), channel_id=1, source_target_pairs={{4,8},{12,16},{20,24},{28,0},{5,9},{13,17},{21,25},{29,1},{6,10},{... | collective-permute-start | bytes 516104 | tf_op jit(solution)/shard_map/cond/branch_7_fun/ppermute | solution.py:430
  7.3 6.5 %collective-permute-start.30 = (f32[7,3,8,128]{3,2,1,0:T(8,128)S(1)}, f32[7,3,8,128]{3,2,1,0:T(8,128)S(1)}, u32[]{:S(2)}, u32[]{:S(2)}) collective-permute-start(f32[7,3,8,128]{3,2,1,0:T(8,128)S(1)} %get-tuple-element.187), channel_id=1, source_target_pairs={{0,1},{4,5},{8,9},{12,13},{16,17},{20,21},{24,25},{28,29},{2,3},{6... | collective-permute-start | bytes 258056 | tf_op jit(solution)/shard_map/cond/branch_7_fun/ppermute | solution.py:430
  8.9 7.5 %collective-permute-start.31 = (f32[7,3,8,128]{3,2,1,0:T(8,128)S(1)}, f32[7,3,8,128]{3,2,1,0:T(8,128)S(1)}, u32[]{:S(2)}, u32[]{:S(2)}) collective-permute-start(f32[7,3,8,128]{3,2,1,0:T(8,128)S(1)} %get-tuple-element.188), channel_id=1, source_target_pairs={{1,2},{5,6},{9,10},{13,14},{17,18},{21,22},{25,26},{29,30},{31,0},... | collective-permute-start | bytes 258056 | tf_op jit(solution)/shard_map/cond/branch_7_fun/ppermute | solution.py:430
  16.4 5.7 %collective-permute-start.32 = (f32[160,128]{1,0:T(8,128)S(1)}, f32[160,128]{1,0:T(8,128)S(1)}, u32[]{:S(2)}, u32[]{:S(2)}) collective-permute-start(f32[160,128]{1,0:T(8,128)S(1)} %get-tuple-element.216), channel_id=1, source_target_pairs={{0,4},{4,8},{8,12},{12,16},{16,20},{20,24},{24,28},{28,0},{1,5},{5... | collective-permute-start | bytes 245768 | tf_op jit(solution)/shard_map/ppermute | solution.py:430
  16.5 5.6 %collective-permute-start.33 = (f32[160,128]{1,0:T(8,128)S(1)}, f32[160,128]{1,0:T(8,128)S(1)}, u32[]{:S(2)}, u32[]{:S(2)}) collective-permute-start(f32[160,128]{1,0:T(8,128)S(1)} %get-tuple-element.217), channel_id=1, source_target_pairs={{0,28},{4,0},{8,4},{12,8},{16,12},{20,16},{24,20},{28,24},{1,29},{... | collective-permute-start | bytes 245768 | tf_op jit(solution)/shard_map/ppermute | solution.py:430

commit v2 on v1

--- a/solution.py
+++ b/solution.py
@@ -15,6 +15,8 @@
 PLAIN = (2, 5, 6)
 SHEAR_Z = (1, 2, 4, 5)
 ROW = 8
+CORNER = 10**10
+EARLY = 4
 TALL = 24
 VMEM = 32 * 1024 * 1024
 
@@ -146,42 +148,49 @@
         pl.when(x_odd == 1)(functools.partial(planes, x_far, x_near))
 
 
+def own_z_kernel(cells_x, state, weights, dz, dzz):
+    got = along_z(state[...].reshape(7 * cells_x * 8, LANES), weights[...])
+    dz[...] = (got[:, :LANES] * (1.0 / 60.0)).reshape(7, cells_x, 8, LANES)
+    dzz[...] = (got[: 5 * cells_x * 8, LANES:] * (1.0 / 180.0)).reshape(5, cells_x, 8, LANES)
+
+
 def side_kernel(
-    cells_x, state, weights, y_near, y_far, dz, mixes, side_terms, block, z_block, dzz
+    cells_x, state, weights, y_near, y_far, dz, dzz, mixes, side_terms, block, z_block
 ):
     own = slice(ROW, ROW + 8)
     y_odd = lax.axis_index("yz") % 2
-    for field in range(7):
-        got = along_z(state[field].reshape(cells_x * 8, LANES), weights[...])
-        dz[field] = (got[:, :LANES] * (1.0 / 60.0)).reshape(cells_x, 8, LANES)
-        if field < 5:
-            dzz[field] = (got[:, LANES:] * (1.0 / 180.0)).reshape(cells_x, 8, LANES)
-        block[field, :, own] = state[field]
+    block[:, :, own] = state[...]
     for number, field in enumerate(SHEAR_Z):
         z_block[number, :, own] = dz[field]
-
-    def ghosts(target, rows):
+    count = 3 * cells_x
+    got = along_z(
+        jnp.concatenate(
+            [rows[field * count : (field + 1) * count] for rows in (y_near, y_far) for field in SHEAR_Z]
+        ),
+        weights[:, :LANES],
+    ) * (1.0 / 60.0)
+
+    def ghosts(target, rows, begin):
         for field in range(7):
             for plane in range(cells_x):
                 at = 3 * (field * cells_x + plane)
                 block[field, plane, target : target + 3] = rows[at : at + 3]
-        got = along_z(rows[...], weights[:, :LANES]) * (1.0 / 60.0)
-        for number, field in enumerate(SHEAR_Z):
+        for number in range(4):
             for plane in range(cells_x):
-                at = 3 * (field * cells_x + plane)
+                at = begin + 3 * (number * cells_x + plane)
                 z_block[number, plane, target : target + 3] = got[at : at + 3]
 
     @pl.when(y_odd == 0)
     def _():
-        ghosts(ROW + 8, y_near)
-        ghosts(ROW - 3, y_far)
+        ghosts(ROW + 8, y_near, 0)
+        ghosts(ROW - 3, y_far, 4 * count)
 
     @pl.when(y_odd == 1)
     def _():
-        ghosts(ROW - 3, y_near)
-        ghosts(ROW + 8, y_far)
-
-    def yz_step(plane, carry):
+        ghosts(ROW - 3, y_near, 0)
+        ghosts(ROW + 8, y_far, 4 * count)
+
+    def yz_step(plane):
         def rows_of(field):
             return lambda step: block[field, plane, ROW + step : ROW + 8 + step]
 
@@ -206,9 +215,17 @@
         mixes[3, plane] = grad[4] + dz[5, plane]
         mixes[4, plane] = grad[3]
         mixes[5, plane] = dz[3, plane]
+
+    in_pairs(0, cells_x, yz_step)
+
+
+def in_pairs(begin, end, step):
+    def two(number, carry):
+        step(begin + 2 * number)
+        step(begin + 2 * number + 1)
         return carry
 
-    lax.fori_loop(0, cells_x, yz_step, 0)
+    lax.fori_loop(0, (end - begin) // 2, two, 0)
 
 
 def corner_kernel(slabs_x, x_near, x_far, after, faces, to_next, to_last):
@@ -259,57 +276,68 @@
 def inner_kernel(
     cells_x, inv_width,
     state, register, forcing, dz, mixes, side_terms,
-    new_state, new_register,
+    new_state, new_register, late_state, late_register,
     fresh_state, fresh_register, sems,
 ):
     first = lax.axis_index("gx") * cells_x
-
-    def plane_step(plane, carry):
-        states, registers = finish(
-            inv_width,
-            first + plane,
-            [state[field, plane] for field in range(7)],
-            [forcing[comp, plane] for comp in range(3)],
-            [register[field, plane] for field in range(7)],
-            x_terms(
-                lambda field: lambda step: state[field, plane + step],
-                lambda number: lambda step: mixes[number, plane + step],
-            ),
-            [side_terms[number, plane] for number in range(13)],
-            [dz[field, plane] for field in range(7)],
-        )
-        for field in range(7):
-            fresh_register[field, plane] = registers[field]
-            fresh_state[field, plane] = states[field]
-        return carry
-
-    middle = cells_x // 2
-    copies = []
-    for number, (begin, end) in enumerate(((3, middle), (middle, cells_x - 3))):
-        lax.fori_loop(begin, end, plane_step, 0)
-        for which, (fresh, final) in enumerate(((fresh_state, new_state), (fresh_register, new_register))):
-            copy = pltpu.make_async_copy(
-                fresh.at[:, pl.ds(begin, end - begin)],
-                final.at[:, pl.ds(begin, end - begin)],
-                sems.at[2 * number + which],
+    early = EARLY
+
+    def step_into(states_out, registers_out, begin):
+        def plane_step(plane):
+            states, registers = finish(
+                inv_width,
+                first + plane,
+                [state[field, plane] for field in range(7)],
+                [forcing[comp, plane] for comp in range(3)],
+                [register[field, plane] for field in range(7)],
+                x_terms(
+                    lambda field: lambda step: state[field, plane + step],
+                    lambda number: lambda step: mixes[number, plane + step],
+                ),
+                [side_terms[number, plane] for number in range(13)],
+                [dz[field, plane] for field in range(7)],
             )
-            copy.start()
-            copies.append(copy)
+            for field in range(7):
+                registers_out[field, plane - begin] = registers[field]
+                states_out[field, plane - begin] = states[field]
+
+        return plane_step
+
+    in_pairs(3, 3 + early, step_into(fresh_state, fresh_register, 3))
+    copies = [
+        pltpu.make_async_copy(fresh, final.at[:, pl.ds(3, early)], sems.at[which])
+        for which, (fresh, final) in enumerate(((fresh_state, new_state), (fresh_register, new_register)))
+    ]
+    for copy in copies:
+        copy.start()
+    in_pairs(3 + early, cells_x - 3, step_into(late_state, late_register, 3 + early))
     for copy in copies:
         copy.wait()
 
 
 def edge_kernel(
-    cells_x, slabs_x, slabs_y, cells_y, inv_width,
+    cells_x, slabs_x, cells_y, inv_width,
     y_shift, state, register, forcing, weights, dz, mixes, side_terms,
-    planes, from_last, from_next, kept_state, kept_register,
+    planes, from_last, from_next, late_state, late_register, kept_state, kept_register,
     new_state, new_register,
-    ghost, faces, face_mixes, fresh_state, fresh_register, sems,
+    ghost, fields, mixed, fresh_state, fresh_register, sems,
 ):
+    late = [
+        pltpu.make_async_copy(part, final.at[:, pl.ds(3 + EARLY, cells_x - 6 - EARLY)], sems.at[4 + which])
+        for which, (part, final) in enumerate(((late_state, new_state), (late_register, new_register)))
+    ]
+    for copy in late:
+        copy.start()
     where_x = lax.axis_index("gx")
     first = where_x * cells_x
     lean = (y_shift[0] + cells_y // 2) % cells_y - cells_y // 2
     at_low, at_high = where_x == 0, where_x == slabs_x - 1
+    for field in range(7):
+        fields[0, field, 3:9] = state[field, 0:6]
+        fields[1, field, 0:6] = state[field, cells_x - 6 :]
+    for number in range(6):
+        mixed[0, number, 3:9] = mixes[number, 0:6]
+        mixed[1, number, 0:6] = mixes[number, cells_x - 6 :]
     for side in range(2):
         for number, field in enumerate(MIXED):
             for plane in range(3):
@@ -332,42 +360,55 @@
     pl.when(at_low)(functools.partial(put, 0))
     pl.when(at_high)(functools.partial(put, 1))
     for side, shift in enumerate((jnp.where(at_low, lean, 0), jnp.where(at_high, -lean, 0))):
-        shift = shift + 16
         for field in range(7):
             for plane in range(3):
-                faces[side, field, plane] = ghost[side, field, plane, pl.ds(shift, 8)]
-        got = along_z(
-            jnp.concatenate([faces[side, field].reshape(24, LANES) for field in (0, 2, 3, 5)]),
-            weights[:, :LANES],
-        ) * (1.0 / 60.0)
+                low = ghost[side, field, plane, pl.ds(shift + 13, 8)]
+                if field in MIXED:
+                    high = ghost[side, field, plane, pl.ds(shift + 21, 8)]
+                    ghost[side, field, plane, 0:8] = low
+                    ghost[side, field, plane, 8:16] = high
+                    fields[side, field, plane + 6 * side] = ghost[side, field, plane, 3:11]
+                else:
+                    fields[side, field, plane + 6 * side] = ghost[side, field, plane, pl.ds(shift + 16, 8)]
+    used = (0, 2, 3, 5)
+    got = along_z(
+        jnp.concatenate(
+            [
+                fields[side, field, 6 * side : 6 * side + 3].reshape(24, LANES)
+                for side in range(2)
+                for field in used
+            ]
+        ),
+        weights[:, :LANES],
+    ) * (1.0 / 60.0)
+    for side in range(2):
         for plane in range(3):
             def rows_of(field):
-                return lambda step: ghost[side, field, plane, pl.ds(shift + step, 8)]
-
-            def depth(number):
-                return got[24 * number + 8 * plane : 24 * number + 8 * plane + 8]
-
-            face_mixes[side, 0, plane] = first_diff(rows_of(1)) + depth(1)
-            face_mixes[side, 1, plane] = first_diff(rows_of(0))
-            face_mixes[side, 2, plane] = depth(0)
-            face_mixes[side, 3, plane] = first_diff(rows_of(4)) + depth(3)
-            face_mixes[side, 4, plane] = first_diff(rows_of(3))
-            face_mixes[side, 5, plane] = depth(2)
-
-    copies = []
+                return lambda step: ghost[side, field, plane, 3 + step : 11 + step]
+
+            def depth(field):
+                at = 24 * (4 * side + used.index(field)) + 8 * plane
+                return got[at : at + 8]
+
+            spot = plane + 6 * side
+            mixed[side, 0, spot] = first_diff(rows_of(1)) + depth(2)
+            mixed[side, 1, spot] = first_diff(rows_of(0))
+            mixed[side, 2, spot] = depth(0)
+            mixed[side, 3, spot] = first_diff(rows_of(4)) + depth(5)
+            mixed[side, 4, spot] = first_diff(rows_of(3))
+            mixed[side, 5, spot] = depth(3)
+
+    def copies_of(side):
+        return [
+            pltpu.make_async_copy(
+                fresh.at[side], final.at[:, pl.ds(side * (cells_x - 3), 3)], sems.at[2 * side + which]
+            )
+            for which, (fresh, final) in enumerate(((fresh_state, new_state), (fresh_register, new_register)))
+        ]
+
     for side in range(2):
-        begin = side * (cells_x - 3)
         for local in range(3):
-            plane = begin + local
-
-            def at(own, far, number, step):
-                spot = plane + step
-                if spot < 0:
-                    return far[0, number, spot + 3]
-                if spot >= cells_x:
-                    return far[1, number, spot - cells_x]
-                return own[number, spot]
-
+            plane = side * (cells_x - 3) + local
             states, registers = finish(
                 inv_width,
                 first + plane,
@@ -375,8 +416,8 @@
                 [forcing[comp, plane] for comp in range(3)],
                 [register[field, plane] for field in range(7)],
                 x_terms(
-                    lambda field: lambda step: at(state, faces, field, step),
-                    lambda number: lambda step: at(mixes, face_mixes, number, step),
+                    lambda field: lambda step: fields[side, field, local + 3 + step],
+                    lambda number: lambda step: mixed[side, number, local + 3 + step],
                 ),
                 [side_terms[number, plane] for number in range(13)],
                 [dz[field, plane] for field in range(7)],
@@ -384,13 +425,9 @@
             for field in range(7):
                 fresh_register[side, field, local] = registers[field]
                 fresh_state[side, field, local] = states[field]
-        for which, (fresh, final) in enumerate(((fresh_state, new_state), (fresh_register, new_register))):
-            copy = pltpu.make_async_copy(
-                fresh.at[side], final.at[:, pl.ds(begin, 3)], sems.at[2 * side + which]
-            )
+        for copy in copies_of(side):
             copy.start()
-            copies.append(copy)
-    for copy in copies:
+    for copy in late + copies_of(0) + copies_of(1):
         copy.wait()
 
 
@@ -415,11 +452,11 @@
             shape(21 * cells_x, LANES), shape(21 * cells_x, LANES),
             shape(7, 3, cells_y, LANES), shape(7, 3, cells_y, LANES),
         ],
-        in_specs=[anyspace],
+        in_specs=[pl.BlockSpec(memory_space=pltpu.HBM)],
         out_specs=[vmem] * 5,
         scratch_shapes=[pltpu.SemaphoreType.DMA((7,))],
         compiler_params=params,
-    )(state)
+    )(pltpu.with_memory_space_constraint(state, pltpu.HBM))
 
     digit = min(slabs_y, 8)
 
@@ -460,78 +497,89 @@
             hop *= 2
         x_far = jnp.where(at_low | at_high, across, x_far)
 
+    beside = [
+        [(place(slab, j), place(slab, j + along)) for slab in range(slabs_x) for j in range(slabs_y)]
+        for along in (1, -1)
+    ]
+
+    def cost(flops):
+        return pl.CostEstimate(flops=flops, bytes_accessed=10**6, transcendentals=0)
+
     def exchange(by, operands):
-        y_near, y_far, x_near, x_far, state, weights = operands
+        y_near, y_far, x_near, x_far, state, register, forcing, weights, y_shift = operands
+        plane = state.shape[1:]
+        x_far = send(x_far, x_pairs(1, by))
+        x_near = send(x_near, x_pairs(0, 0))
         y_near = send(y_near, y_pairs(0))
-        x_near = send(x_near, x_pairs(0, 0))
-        x_far = send(x_far, x_pairs(1, by))
         y_far = send(y_far, y_pairs(1))
-        terms = pl.pallas_call(
-            functools.partial(side_kernel, cells_x),
-            out_shape=[shape(*state.shape), shape(6, *state.shape[1:]), shape(13, *state.shape[1:])],
-            in_specs=[vmem] * 4,
-            out_specs=[vmem] * 3,
-            scratch_shapes=[
-                pltpu.VMEM((7, cells_x, TALL, LANES), jnp.float32),
-                pltpu.VMEM((4, cells_x, TALL, LANES), jnp.float32),
-                pltpu.VMEM((5, *state.shape[1:]), jnp.float32),
-            ],
+        dz, dzz = pl.pallas_call(
+            functools.partial(own_z_kernel, cells_x),
+            out_shape=[shape(7, *plane), shape(5, *plane)],
+            in_specs=[vmem] * 2,
+            out_specs=[vmem] * 2,
             compiler_params=params,
-            cost_estimate=pl.CostEstimate(flops=2 * 10**8, bytes_accessed=10**6, transcendentals=0),
-        )(state, weights, y_near, y_far)
-        corners = pl.pallas_call(
+            cost_estimate=cost(10**8),
+        )(state, weights)
+        faces, to_next, to_last = pl.pallas_call(
             functools.partial(corner_kernel, slabs_x),
             out_shape=[shape(2, *x_near.shape), shape(160, LANES), shape(160, LANES)],
             in_specs=[vmem] * 2 + [anyspace],
             out_specs=[vmem] * 3,
             compiler_params=params,
-        )(x_near, x_far, terms[2])
-        return (*terms, *corners)
-
-    dz, mixes, side_terms, faces, to_next, to_last = lax.switch(
+            cost_estimate=cost(CORNER),
+        )(x_near, x_far, dz)
+        from_last = send(to_next, beside[0])
+        from_next = send(to_last, beside[1])
+        mixes, side_terms = pl.pallas_call(
+            functools.partial(side_kernel, cells_x),
+            out_shape=[shape(6, *plane), shape(13, *plane)],
+            in_specs=[vmem] * 6,
+            out_specs=[vmem] * 2,
+            scratch_shapes=[
+                pltpu.VMEM((7, cells_x, TALL, LANES), jnp.float32),
+                pltpu.VMEM((4, cells_x, TALL, LANES), jnp.float32),
+            ],
+            compiler_params=params,
+            cost_estimate=cost(2 * 10**8),
+        )(state, weights, y_near, y_far, dz, dzz)
+        early, late = EARLY, cells_x - 6 - EARLY
+        new_state, new_register, late_state, late_register = pl.pallas_call(
+            functools.partial(inner_kernel, cells_x, 1.0 / total_x),
+            out_shape=[shape(*state.shape)] * 2 + [shape(7, late, *plane[1:])] * 2,
+            in_specs=[vmem] * 6,
+            out_specs=[anyspace] * 2 + [vmem] * 2,
+            scratch_shapes=[
+                pltpu.VMEM((7, early, *plane[1:]), jnp.float32),
+                pltpu.VMEM((7, early, *plane[1:]), jnp.float32),
+                pltpu.SemaphoreType.DMA((2,)),
+            ],
+            compiler_params=params,
+            cost_estimate=cost(2 * 10**8),
+        )(state, register, forcing, dz, mixes, side_terms)
+        return pl.pallas_call(
+            functools.partial(edge_kernel, cells_x, slabs_x, cells_y, 1.0 / total_x),
+            out_shape=[shape(*state.shape)] * 2,
+            in_specs=[smem] + [vmem] * 12 + [anyspace] * 2,
+            out_specs=[anyspace] * 2,
+            input_output_aliases={13: 0, 14: 1},
+            scratch_shapes=[
+                pltpu.VMEM((2, 7, 3, 40, LANES), jnp.float32),
+                pltpu.VMEM((2, 7, 9, 8, LANES), jnp.float32),
+                pltpu.VMEM((2, 6, 9, 8, LANES), jnp.float32),
+                pltpu.VMEM((2, 7, 3, 8, LANES), jnp.float32),
+                pltpu.VMEM((2, 7, 3, 8, LANES), jnp.float32),
+                pltpu.SemaphoreType.DMA((6,)),
+            ],
+            compiler_params=params,
+        )(
+            y_shift, state, register, forcing, weights, dz, mixes, side_terms,
+            faces, from_last, from_next, late_state, late_register, new_state, new_register,
+        )
+
+    return lax.switch(
         steps % digit,
         [functools.partial(exchange, by) for by in range(digit)],
-        (y_near, y_far, x_near, x_far, held, weights),
-    )
-    beside = [
-        [(place(slab, j), place(slab, j + along)) for slab in range(slabs_x) for j in range(slabs_y)]
-        for along in (1, -1)
-    ]
-    from_last = send(to_next, beside[0])
-    from_next = send(to_last, beside[1])
-
-    new_state, new_register = pl.pallas_call(
-        functools.partial(inner_kernel, cells_x, 1.0 / total_x),
-        out_shape=[shape(*state.shape)] * 2,
-        in_specs=[vmem] * 6,
-        out_specs=[anyspace] * 2,
-        scratch_shapes=[
-            pltpu.VMEM(state.shape, jnp.float32),
-            pltpu.VMEM(state.shape, jnp.float32),
-            pltpu.SemaphoreType.DMA((4,)),
-        ],
-        compiler_params=params,
-        cost_estimate=pl.CostEstimate(flops=2 * 10**8, bytes_accessed=2 * 10**6, transcendentals=0),
-    )(held, register, forcing, dz, mixes, side_terms)
-
-    return pl.pallas_call(
-        functools.partial(edge_kernel, cells_x, slabs_x, slabs_y, cells_y, 1.0 / total_x),
-        out_shape=[shape(*state.shape)] * 2,
-        in_specs=[smem] + [vmem] * 10 + [anyspace] * 2,
-        out_specs=[anyspace] * 2,
-        input_output_aliases={11: 0, 12: 1},
-        scratch_shapes=[
-            pltpu.VMEM((2, 7, 3, 40, LANES), jnp.float32),
-            pltpu.VMEM((2, 7, 3, 8, LANES), jnp.float32),
-            pltpu.VMEM((2, 6, 3, 8, LANES), jnp.float32),
-            pltpu.VMEM((2, 7, 3, 8, LANES), jnp.float32),
-            pltpu.VMEM((2, 7, 3, 8, LANES), jnp.float32),
-            pltpu.SemaphoreType.DMA((4,)),
-        ],
-        compiler_params=params,
-    )(
-        y_shift, held, register, forcing, weights, dz, mixes, side_terms,
-        faces, from_last, from_next, new_state, new_register,
+        (y_near, y_far, x_near, x_far, held, register, forcing, weights, y_shift),
     )
 
 

time: 24.7 us -> 22 us (0.89); the launches traced: 24.4 us -> 22.3 us
  Pallas kernels: 7.87 us -> 6.13 us
  local copies, waits for them, and re-layouts: 1.11 us -> 0.01 us
  starting transfers between devices: 10.1 us -> 10.8 us
  waiting for transfers between devices: 3.96 us -> 3.26 us
  loops' own time: 0.01 us -> 0.52 us
    pallas_call x1, Pallas kernels: 2.32 us -> 1 us  [exchange(): pl.pallas_call(functools.partial(side_kernel, cells_x), out_shape=[shape(...]
    unnamed x8 -> x2, local copies, waits for them, and re-layouts: 1.11 us -> 0.01 us
    pallas_call x2 -> x3, Pallas kernels: 4.7 us -> 3.97 us  [the longest x1 1.87 us: exchange(): pl.pallas_call(functools.partial(edge_kernel, cells_x, slabs_x, cells_y,...]
    ppermute x6, waiting for transfers between devices: 3.96 us -> 3.26 us  [send(): return lax.ppermute(value, ('yz', 'gx'), pairs)]
    ppermute x6, starting transfers between devices: 10.1 us -> 10.8 us  [send(): return lax.ppermute(value, ('yz', 'gx'), pairs)]
    another operation x1, loops' own time: 0.01 us -> 0.52 us  [per_device(): lax.switch(steps % digit, [functools.partial(exchange, by) for by in rang...]
    pallas_call x1, Pallas kernels: 0.8 us -> 1.11 us  [per_device(): pl.pallas_call(functools.partial(pack_kernel, cells_x, cells_y), out_shap...]
  transfers between devices with their start and end apart: 6 -> 6, of which waited for: 3 -> 2; matrix products, arithmetic and copies ran while one was open for 0% -> 0% of each run, Pallas kernels for 19% -> 14%
where the time goes in v2:
time: 22 us; the launch traced here: 22.3 us
  starting transfers between devices  10.8 us (49%)
  Pallas kernels  6.13 us (28%)
  waiting for transfers between devices  3.26 us (15%)
  between operations  1.57 us (7%)
  loops' own time  0.52 us (2%)
    ppermute x6, starting transfers between devices, send(): return lax.ppermute(value, ('yz', 'gx'), pairs)  10.8 us
    ppermute x6, waiting for transfers between devices, send(): return lax.ppermute(value, ('yz', 'gx'), pairs)  3.26 us
    pallas_call x1, Pallas kernels, exchange(): pl.pallas_call(functools.partial(edge_kernel, cells_x, slabs_x, cells_y,...  1.87 us
    pallas_call x1, Pallas kernels, exchange(): pl.pallas_call(functools.partial(own_z_kernel, cells_x), out_shape=[shape...  1.19 us
    pallas_call x1, Pallas kernels, per_device(): pl.pallas_call(functools.partial(pack_kernel, cells_x, cells_y), out_shap...  1.11 us
    pallas_call x1, Pallas kernels, exchange(): pl.pallas_call(functools.partial(side_kernel, cells_x), out_shape=[shape(...  1 us
    pallas_call x1, Pallas kernels, exchange(): pl.pallas_call(functools.partial(inner_kernel, cells_x, 1.0 / total_x), o...  0.91 us
    another operation x1, loops' own time, per_device(): lax.switch(steps % digit, [functools.partial(exchange, by) for by in rang...  0.52 us
  transfers between devices with their start and end apart: 6, of which 2 were waited for; matrix products, arithmetic and copies ran while one was open for 0% of the time, Pallas kernels for 14%

profile of v2, /device:TPU:0, one launch (start us, length us, event | category | flops | bytes accessed | tf_op | source)
XLA Modules:
  0.0 22.3 jit_solution(14955979019433384932)
XLA Ops:
  0.6 0.0 copy-start
  1.4 1.1 %shard_map.84 = (f32[7,16,8,128]{3,2,1,0:T(8,128)S(1)}, f32[336,128]{1,0:T(8,128)S(1)}, f32[336,128]{1,0:T(8,128)S(1)}, f32[7,3,8,128]{3,2,1,0:T(8,128)S(1)}, f32[7,3,8,128]{3,2,1,0:T(8,128)S(1)}) custom-call(f32[7,16,8,128]{3,2,1,0:T(8,128)} %state.1), custom_call_target="tpu_custom_call" | custom-call | tf_op jit(solution)/shard_map/pallas_call | solution.py:448
  2.5 0.0 copy-done
  2.5 19.6 %conditional.1 = ((f32[7,16,8,128]{3,2,1,0:T(8,128)}, f32[7,16,8,128]{3,2,1,0:T(8,128)})) conditional(s32[]{:T(128)} %clamp.3, (f32[7,16,8,128]{3,2,1,0:T(8,128)S(1)}, bf16[256,256]{1,0:T(8,128)(2,1)}, f32[336,128]{1,0:T(8,128)S(1)}, f32[336,128]{1,0:T(8,128)S(1)}, f32[7,3,8,128]{3,2,1,0:T(8,128)S(1)}, ...), branch_computations={%region_0.1_spmd, %region_1.2_spmd, %region_2.3_spmd, %region_3.4_... | conditional | flops 10499999744 | bytes 8030768 | solution.py:579
  2.7 3.1 %collective-permute-start.38 = (f32[7,3,8,128]{3,2,1,0:T(8,128)S(1)}, f32[7,3,8,128]{3,2,1,0:T(8,128)S(1)}, u32[]{:S(2)}, u32[]{:S(2)}) collective-permute-start(f32[7,3,8,128]{3,2,1,0:T(8,128)S(1)} %get-tuple-element.275), channel_id=1, source_target_pairs={{0,1},{4,5},{8,9},{12,13},{16,17},{20,21},{24,25},{28,29},{2,3},{6... | collective-permute-start | bytes 258056 | tf_op jit(solution)/shard_map/cond/branch_6_fun/ppermute | solution.py:467
  5.8 4.4 %collective-permute-start.39 = (f32[7,3,8,128]{3,2,1,0:T(8,128)S(1)}, f32[7,3,8,128]{3,2,1,0:T(8,128)S(1)}, u32[]{:S(2)}, u32[]{:S(2)}) collective-permute-start(f32[7,3,8,128]{3,2,1,0:T(8,128)S(1)} %get-tuple-element.276), channel_id=1, source_target_pairs={{1,2},{5,6},{9,10},{13,14},{17,18},{21,22},{25,26},{29,30},{27,0},... | collective-permute-start | bytes 258056 | tf_op jit(solution)/shard_map/cond/branch_6_fun/ppermute | solution.py:467
  10.2 0.0 collective-permute-start.36
  10.2 0.6 %collective-permute-start.37 = (f32[336,128]{1,0:T(8,128)S(1)}, f32[336,128]{1,0:T(8,128)S(1)}, u32[]{:S(2)}, u32[]{:S(2)}) collective-permute-start(f32[336,128]{1,0:T(8,128)S(1)} %get-tuple-element.271), channel_id=1, source_target_pairs={{4,8},{12,16},{20,24},{28,0},{5,9},{13,17},{21,25},{29,1},{6,10},{... | collective-permute-start | bytes 516104 | tf_op jit(solution)/shard_map/cond/branch_6_fun/ppermute | solution.py:467
  10.8 1.2 %branch_6_fun.5 = (f32[7,16,8,128]{3,2,1,0:T(8,128)S(1)}, f32[5,16,8,128]{3,2,1,0:T(8,128)S(1)}) custom-call(f32[7,16,8,128]{3,2,1,0:T(8,128)S(1)} %get-tuple-element.265.state, bf16[256,256]{1,0:T(8,128)(2,1)} %get-tuple-element.268.weights), custom_call_target="tpu_custom_call" | custom-call | flops 100000000 | bytes 1000000 | tf_op jit(solution)/shard_map/cond/branch_6_fun/pallas_call | solution.py:515
  12.0 0.0 collective-permute-done.38.x_near
  12.0 2.4 %collective-permute-done.39.x_far = f32[7,3,8,128]{3,2,1,0:T(8,128)S(1)} collective-permute-done((f32[7,3,8,128]{3,2,1,0:T(8,128)S(1)}, f32[7,3,8,128]{3,2,1,0:T(8,128)S(1)}, u32[]{:S(2)}, u32[]{:S(2)}) %collective-permute-start.39) | collective-permute-done | bytes 86048 | tf_op jit(solution)/shard_map/cond/branch_6_fun/ppermute | solution.py:467
  14.4 0.0 copy-start.7
  14.4 0.1 branch_6_fun.7
  14.5 0.1 collective-permute-start.40
  14.6 2.6 %collective-permute-start.41 = (f32[160,128]{1,0:T(8,128)S(1)}, f32[160,128]{1,0:T(8,128)S(1)}, u32[]{:S(2)}, u32[]{:S(2)}) collective-permute-start(f32[160,128]{1,0:T(8,128)S(1)} %get-tuple-element.279), channel_id=1, source_target_pairs={{0,28},{4,0},{8,4},{12,8},{16,12},{20,16},{24,20},{28,24},{1,29},{... | collective-permute-start | bytes 245768 | tf_op jit(solution)/shard_map/cond/branch_6_fun/ppermute | solution.py:467
  17.2 0.0 collective-permute-done.36.y_near
  17.2 0.9 %collective-permute-done.37.y_far = f32[336,128]{1,0:T(8,128)S(1)} collective-permute-done((f32[336,128]{1,0:T(8,128)S(1)}, f32[336,128]{1,0:T(8,128)S(1)}, u32[]{:S(2)}, u32[]{:S(2)}) %collective-permute-start.37) | collective-permute-done | bytes 172064 | tf_op jit(solution)/shard_map/cond/branch_6_fun/ppermute | solution.py:467
  18.1 0.0 copy-done.7
  18.1 0.0 copy-start.15
  18.1 1.0 %branch_6_fun.6 = (f32[6,16,8,128]{3,2,1,0:T(8,128)S(1)}, f32[13,16,8,128]{3,2,1,0:T(8,128)S(1)}) custom-call(f32[7,16,8,128]{3,2,1,0:T(8,128)S(1)} %get-tuple-element.265.state, bf16[256,256]{1,0:T(8,128)(2,1)S(1)} %copy-done.7, f32[336,128]{1,0:T(8,128)S(1)} %collective-permute-done.36.y_near, f32[336,128]{1,0:T(8,128)S(1)} %collective-permute-done.37.y_far, ...), custom_call_target="tpu_custom_call" | custom-call | flops 200000000 | bytes 1000000 | tf_op jit(solution)/shard_map/cond/branch_6_fun/pallas_call | solution.py:533
  19.1 0.0 copy-done.15
  19.1 0.9 %branch_6_fun.8 = (f32[7,16,8,128]{3,2,1,0:T(8,128)}, f32[7,16,8,128]{3,2,1,0:T(8,128)}, f32[7,6,8,128]{3,2,1,0:T(8,128)S(1)}, f32[7,6,8,128]{3,2,1,0:T(8,128)S(1)}) custom-call(f32[7,16,8,128]{3,2,1,0:T(8,128)S(1)} %get-tuple-element.265.state, f32[7,16,8,128]{3,2,1,0:T(8,128)S(1)} %get-tuple-element.266.register, f32[3,16,8,128]{3,2,1,0:T(8,128)S(1)} %copy-done.15, ...), custom_call_target="tpu_custom_call" | custom-call | flops 200000000 | bytes 1000000 | tf_op jit(solution)/shard_map/cond/branch_6_fun/pallas_call | solution.py:546
  20.0 0.0 collective-permute-done.40.from_last
  20.0 0.0 collective-permute-done.41.from_next
  20.0 1.9 %branch_6_fun.9 = (f32[7,16,8,128]{3,2,1,0:T(8,128)}, f32[7,16,8,128]{3,2,1,0:T(8,128)}) custom-call(s32[1]{0:T(128)} %get-tuple-element.264.y_shift, f32[7,16,8,128]{3,2,1,0:T(8,128)S(1)} %get-tuple-element.265.state, f32[7,16,8,128]{3,2,1,0:T(8,128)S(1)} %get-tuple-element.266.register, ...), custom_call_target="tpu_custom_call", output_to_operand_aliasing={{0}: (13, {}), {1}: (14, {})} | custom-call | tf_op jit(solution)/shard_map/cond/branch_6_fun/pallas_call | solution.py:559
Async XLA Ops:
  0.6 1.9 %copy-start = (f32[7,16,8,128]{3,2,1,0:T(8,128)S(1)}, f32[7,16,8,128]{3,2,1,0:T(8,128)}, u32[]{:S(2)}) copy-start(f32[7,16,8,128]{3,2,1,0:T(8,128)} %param.14) | copy-start | bytes 1376260
  2.7 9.3 %collective-permute-start.38 = (f32[7,3,8,128]{3,2,1,0:T(8,128)S(1)}, f32[7,3,8,128]{3,2,1,0:T(8,128)S(1)}, u32[]{:S(2)}, u32[]{:S(2)}) collective-permute-start(f32[7,3,8,128]{3,2,1,0:T(8,128)S(1)} %get-tuple-element.275), channel_id=1, source_target_pairs={{0,1},{4,5},{8,9},{12,13},{16,17},{20,21},{24,25},{28,29},{2,3},{6... | collective-permute-start | bytes 258056 | tf_op jit(solution)/shard_map/cond/branch_6_fun/ppermute | solution.py:467
  5.8 8.6 %collective-permute-start.39 = (f32[7,3,8,128]{3,2,1,0:T(8,128)S(1)}, f32[7,3,8,128]{3,2,1,0:T(8,128)S(1)}, u32[]{:S(2)}, u32[]{:S(2)}) collective-permute-start(f32[7,3,8,128]{3,2,1,0:T(8,128)S(1)} %get-tuple-element.276), channel_id=1, source_target_pairs={{1,2},{5,6},{9,10},{13,14},{17,18},{21,22},{25,26},{29,30},{27,0},... | collective-permute-start | bytes 258056 | tf_op jit(solution)/shard_map/cond/branch_6_fun/ppermute | solution.py:467
  10.2 7.0 %collective-permute-start.36 = (f32[336,128]{1,0:T(8,128)S(1)}, f32[336,128]{1,0:T(8,128)S(1)}, u32[]{:S(2)}, u32[]{:S(2)}) collective-permute-start(f32[336,128]{1,0:T(8,128)S(1)} %get-tuple-element.270), channel_id=1, source_target_pairs={{0,4},{8,12},{16,20},{24,28},{1,5},{9,13},{17,21},{25,29},{2,6},{1... | collective-permute-start | bytes 516104 | tf_op jit(solution)/shard_map/cond/branch_6_fun/ppermute | solution.py:467
  10.2 7.9 %collective-permute-start.37 = (f32[336,128]{1,0:T(8,128)S(1)}, f32[336,128]{1,0:T(8,128)S(1)}, u32[]{:S(2)}, u32[]{:S(2)}) collective-permute-start(f32[336,128]{1,0:T(8,128)S(1)} %get-tuple-element.271), channel_id=1, source_target_pairs={{4,8},{12,16},{20,24},{28,0},{5,9},{13,17},{21,25},{29,1},{6,10},{... | collective-permute-start | bytes 516104 | tf_op jit(solution)/shard_map/cond/branch_6_fun/ppermute | solution.py:467
  14.4 3.6 %copy-start.7 = (bf16[256,256]{1,0:T(8,128)(2,1)S(1)}, bf16[256,256]{1,0:T(8,128)(2,1)}, u32[]{:S(2)}) copy-start(bf16[256,256]{1,0:T(8,128)(2,1)} %get-tuple-element.268.weights) | copy-start | bytes 393220 | tf_op jit(solution)/shard_map/cond
  14.5 5.5 %collective-permute-start.40 = (f32[160,128]{1,0:T(8,128)S(1)}, f32[160,128]{1,0:T(8,128)S(1)}, u32[]{:S(2)}, u32[]{:S(2)}) collective-permute-start(f32[160,128]{1,0:T(8,128)S(1)} %get-tuple-element.278), channel_id=1, source_target_pairs={{0,4},{4,8},{8,12},{12,16},{16,20},{20,24},{24,28},{28,0},{1,5},{5... | collective-permute-start | bytes 245768 | tf_op jit(solution)/shard_map/cond/branch_6_fun/ppermute | solution.py:467
  14.6 5.4 %collective-permute-start.41 = (f32[160,128]{1,0:T(8,128)S(1)}, f32[160,128]{1,0:T(8,128)S(1)}, u32[]{:S(2)}, u32[]{:S(2)}) collective-permute-start(f32[160,128]{1,0:T(8,128)S(1)} %get-tuple-element.279), channel_id=1, source_target_pairs={{0,28},{4,0},{8,4},{12,8},{16,12},{20,16},{24,20},{28,24},{1,29},{... | collective-permute-start | bytes 245768 | tf_op jit(solution)/shard_map/cond/branch_6_fun/ppermute | solution.py:467
  18.1 1.0 %copy-start.15 = (f32[3,16,8,128]{3,2,1,0:T(8,128)S(1)}, f32[3,16,8,128]{3,2,1,0:T(8,128)}, u32[]{:S(2)}) copy-start(f32[3,16,8,128]{3,2,1,0:T(8,128)} %get-tuple-element.267.forcing) | copy-start | bytes 589828 | tf_op jit(solution)/shard_map/cond
